TPU v7x, 32 devices: a whole 2x2x4 slice. The times are simulated.
32 devices in a mesh: row: 4 (over x, core), col: 2 (over y), layer: 4 (over z).
Axes of the slice: x: 2, y: 2, z: 4, core: 2. Of those that a mesh axis runs over, the one named last changes fastest.
Arguments:
- a_values: float32 [4, 2, 4, 2, 8, 64, 64], P('row', 'col', 'layer'), may hold values from -6 to 6
- a_places: int32 [4, 2, 4, 2, 8, 2], P('row', 'col', 'layer'), may hold values from 0 to 7, as said below
- a_counts: int32 [4, 2, 4, 2], P('row', 'col', 'layer'), may hold values from 2 to 8, as said below
- b_values: float32 [4, 2, 4, 24, 64, 64], P('row', 'col', 'layer'), may hold values from -0.375 to 0.375
- b_places: int32 [4, 2, 4, 24, 2], P('row', 'col', 'layer'), may hold values from 0 to 15, as said below
- b_counts: int32 [4, 2, 4], P('row', 'col', 'layer'), may hold values from 6 to 24, as said below
Outputs:
- product: float32 [2048, 2048], P(('row', 'layer'), 'col')
Inputs may be any that keep to these rules, and one draw needn't show every extreme that they name: a_places[..., 0] lies below 8 and a_places[..., 1] below 2; within one tile the slots name distinct positions. b_places[..., 0] lies below 2 and b_places[..., 1] below 16; within one tile the slots name distinct positions. `a_counts`: some tile is full. `b_counts`: some tile is full.
All inputs are finite; a program needn't handle non-finite values.
Results may differ from a plain program's by a relative error of at most 0.00007.
Values sent between devices are 32-bit elements; how exact they have to be, the bound alone decides.
A program may use at most 64 MiB of HBM per device.

v0:
```python
import jax
import jax.numpy as jnp
from jax import lax
from jax.sharding import PartitionSpec as P

TILE_ROWS = 8


def from_behind(block, axis, distance):
    devices = range(lax.axis_size(axis))
    route = [((i - distance) % len(devices), i) for i in devices]
    return lax.ppermute(block, axis, route)


def densify(values, places, count, rows, cols):
    slots = values.shape[0]
    width = values.shape[1]
    live = jnp.arange(slots, dtype=jnp.int32) < count
    spots = places[:, 0] * cols + places[:, 1]
    target = jnp.arange(rows * cols, dtype=jnp.int32)
    select = ((target[:, None] == spots[None, :]) & live[None, :]).astype(jnp.float32)
    flat = jnp.dot(
        select,
        values.reshape(slots, width * width),
        precision=lax.Precision.HIGHEST,
        preferred_element_type=jnp.float32,
    )
    return (
        flat.reshape(rows, cols, width, width)
        .transpose(0, 2, 1, 3)
        .reshape(rows * width, cols * width)
    )


def body(a_values, a_places, a_counts, b_values, b_places, b_counts):
    a_vals = a_values.reshape(a_values.shape[3:])
    a_pos = a_places.reshape(a_places.shape[3:])
    a_num = a_counts.reshape(a_counts.shape[3:])
    b_vals = b_values.reshape(b_values.shape[3:])
    b_pos = b_places.reshape(b_places.shape[3:])
    b_num = b_counts.reshape((1,))
    rows_grid = lax.axis_size("row")
    cols_grid = lax.axis_size("col")
    layers = lax.axis_size("layer")
    inner = TILE_ROWS // layers
    tile_cols = TILE_ROWS * rows_grid // cols_grid
    width = a_vals.shape[-1]
    my_col = lax.axis_index("col")

    def product(left_vals, left_pos, left_num, right_vals, right_pos, right_num):
        left = densify(left_vals, left_pos, left_num, TILE_ROWS, inner)
        right = densify(right_vals, right_pos, right_num, inner, tile_cols)
        return jnp.dot(
            left, right, precision=lax.Precision.HIGHEST, preferred_element_type=jnp.float32
        )

    start_sum = jnp.zeros((TILE_ROWS * width, tile_cols * width), jnp.float32)

    def advance(step, carry):
        partial_value, av, ap, an, bv, bp, bn = carry
        partial_value = partial_value + product(av[0], ap[0], an[0], bv, bp, bn[0])
        av, ap, an = from_behind((av, ap, an), "col", -1)
        last = my_col == cols_grid - 1
        av = jnp.where(last, jnp.roll(av, -1, 0), av)
        ap = jnp.where(last, jnp.roll(ap, -1, 0), ap)
        an = jnp.where(last, jnp.roll(an, -1, 0), an)
        bv, bp, bn = from_behind((bv, bp, bn), "row", -1)
        return (partial_value, av, ap, an, bv, bp, bn)

    carry = lax.fori_loop(
        0, rows_grid - 1, advance, (start_sum, a_vals, a_pos, a_num, b_vals, b_pos, b_num)
    )
    partial_value, av, ap, an, bv, bp, bn = carry
    partial_value = partial_value + product(av[0], ap[0], an[0], bv, bp, bn[0])
    return lax.psum_scatter(partial_value, "layer", scatter_dimension=0, tiled=True)


def solution(mesh):
    in_specs = (
        P("row", "col", "layer", None, None, None, None),
        P("row", "col", "layer", None, None, None),
        P("row", "col", "layer", None),
        P("row", "col", "layer", None, None, None),
        P("row", "col", "layer", None, None),
        P("row", "col", "layer"),
    )
    out_specs = P(("row", "layer"), "col")
    return jax.shard_map(body, mesh=mesh, in_specs=in_specs, out_specs=out_specs, check_vma=False)
```

profile of v0, /device:TPU:0, one launch (start us, length us, event | category | flops | bytes accessed | tf_op | source)
XLA Modules:
  0.0 172.1 jit_solution(15434714401196545867)
XLA Ops:
  6.5 2.1 %copy.73 = f32[1,1,1,24,64,64]{5,4,3,2,1,0:T(8,128)} copy(f32[1,1,1,24,64,64]{5,4,3,2,1,0:T(8,128)} %param.11) | data formatting | bytes 786432
  12.9 97.4 %while.25 = (s32[]{:T(128)}, f32[512,1024]{1,0:T(8,128)}, f32[2,8,64,64]{3,2,1,0:T(8,128)}, s32[2,8,2]{1,2,0:T(2,128)S(1)}, s32[2]{0:T(128)}, /*index=5*/f32[24,...) while((s32[]{:T(128)}, f32[512,1024]{1,0:T(8,128)}, ...), condition=%wide.region_1.2_spmd.clone, body=%wide.region_0.1_spmd.clone.sunk | while | flops 850528256 | bytes 32247624 | solution.py:70
  12.9 3.0 %collective-permute-start = (f32[2,8,64,64]{3,2,1,0:T(8,128)}, f32[2,8,64,64]{3,2,1,0:T(8,128)}, u32[]{:S(2)}, u32[]{:S(2)}) collective-permute-start(f32[2,8,64,64]{3,2,1,0:T(8,128)} %get-tuple-element.257), channel_id=1, source_target_pairs={{4,0},{0,4},{5,1},{1,5},{6,2},{2,6},{7,3},{3,7},{12,8},{8,12},{13,... | collective-permute-start | bytes 786440 | tf_op jit(solution)/shard_map/while/body/eval_jaxpr/ppermute | solution.py:12
  16.0 1.9 %collective-permute-start.2 = (s32[2]{0:T(128)}, s32[2]{0:T(128)S(1)}, u32[]{:S(2)}, u32[]{:S(2)}) collective-permute-start(s32[2]{0:T(128)} %get-tuple-element.259), channel_id=1, source_target_pairs={{4,0},{0,4},{5,1},{1,5},{6,2},{2,6},{7,3},{3,7},{12,8},{8,12},{13,... | collective-permute-start | bytes 32 | tf_op jit(solution)/shard_map/while/body/eval_jaxpr/ppermute | solution.py:12
  30.3 2.2 %convolution_bitcast_fusion.6 = f32[8,64,2,64]{3,0,1,2:T(8,128)} fusion(f32[64,64,8]{1,0,2:T(8,128)} %dot_general.52, s32[8]{0:T(128)S(1)} %add_bitcast_fusion.6, s32[8,2]{0,1:T(2,128)} %multiply_add_fusion.6, pred[8]{0:T(512)(128)(4,1)S(1)} %iota_compare_fusion.6), kind=kOutput, calls=%fused_computation.2.clone.1 | convolution fusion | flops 6291712 | bytes 393320 | tf_op jit(solution)/shard_map/while/body/eval_jaxpr/dot_general | solution.py:22
  32.5 2.0 %copy.38 = f32[8,64,2,64]{1,0,3,2:T(8,128)} copy(f32[8,64,2,64]{3,0,1,2:T(8,128)} %convolution_bitcast_fusion.6) | data formatting | bytes 524288 | tf_op jit(solution)/shard_map/while/body/eval_jaxpr/transpose | solution.py:30
  34.5 1.9 %reshape.257 = f32[512,128]{0,1:T(8,128)} reshape(f32[8,64,2,64]{1,0,3,2:T(8,128)} %copy.38) | data formatting | bytes 524288 | tf_op jit(solution)/shard_map/while/body/eval_jaxpr/reshape | solution.py:31
  36.4 3.2 %select_add_fusion.2 = f32[512,1024]{1,0:T(8,128)S(1)} fusion(f32[512,1024]{1,0:T(8,128)S(1)} %copy-done, f32[512,128]{0,1:T(8,128)} %reshape.257, f32[128,1024]{1,0:T(8,128)S(1)} %reshape.259, pred[]{:T(512)S(6)} %compare.3), kind=kOutput, calls=%fused_computation.clone.1 | convolution fusion | flops 806354944 | bytes 4980737 | tf_op jit(solution)/shard_map/while/body/eval_jaxpr/dot_general | solution.py:53
  41.7 2.0 %broadcast_select_fusion.2 = s32[2]{0:T(128)} fusion(s32[2]{0:T(128)S(1)} %collective-permute-done.2, pred[]{:T(512)} %get-tuple-element.274, s32[1]{0:T(128)} %get-tuple-element.242, s32[1]{0:T(128)} %get-tuple-element.243), kind=kLoop, calls=%fused_computation.24.clone.1 | loop fusion | flops 4 | bytes 25 | tf_op jit(solution)/shard_map/while/body/eval_jaxpr/jit(_where)/select_n | solution.py:66
  44.8 1.9 %maximum_select_fusion.2 = f32[2,8,64,64]{3,2,1,0:T(8,128)} fusion(f32[2,8,64,64]{3,2,1,0:T(8,128)} %collective-permute-done, f32[1,8,64,64]{3,2,1,0:T(8,128)S(1)} %get-tuple-element.238, f32[1,8,64,64]{3,2,1,0:T(8,128)S(1)} %get-tuple-element.239, pred[]{:T(512)} %get-tuple-element.274), kind=kLoop, calls=%fused_computation.5.clone.1 | loop fusion | flops 131072 | bytes 786433 | tf_op jit(solution)/shard_map/while/body/eval_jaxpr/jit(_where)/select_n | solution.py:64
  47.4 2.0 %collective-permute-start.1 = (s32[2,8,2]{1,2,0:T(2,128)S(1)}, s32[2,8,2]{1,2,0:T(2,128)S(1)}, u32[]{:S(2)}, u32[]{:S(2)}) collective-permute-start(s32[2,8,2]{1,2,0:T(2,128)S(1)} %get-tuple-element.258), channel_id=1, source_target_pairs={{4,0},{0,4},{5,1},{1,5},{6,2},{2,6},{7,3},{3,7},{12,8},{8,12},{13,... | collective-permute-start | bytes 392 | tf_op jit(solution)/shard_map/while/body/eval_jaxpr/ppermute | solution.py:12
  61.0 2.2 %convolution_bitcast_fusion.6 = f32[8,64,2,64]{3,0,1,2:T(8,128)} fusion(f32[64,64,8]{1,0,2:T(8,128)} %dot_general.52, s32[8]{0:T(128)S(1)} %add_bitcast_fusion.6, s32[8,2]{0,1:T(2,128)} %multiply_add_fusion.6, pred[8]{0:T(512)(128)(4,1)S(1)} %iota_compare_fusion.6), kind=kOutput, calls=%fused_computation.2.clone.1 | convolution fusion | flops 6291712 | bytes 393320 | tf_op jit(solution)/shard_map/while/body/eval_jaxpr/dot_general | solution.py:22
  63.2 2.0 %copy.38 = f32[8,64,2,64]{1,0,3,2:T(8,128)} copy(f32[8,64,2,64]{3,0,1,2:T(8,128)} %convolution_bitcast_fusion.6) | data formatting | bytes 524288 | tf_op jit(solution)/shard_map/while/body/eval_jaxpr/transpose | solution.py:30
  65.2 1.9 %reshape.257 = f32[512,128]{0,1:T(8,128)} reshape(f32[8,64,2,64]{1,0,3,2:T(8,128)} %copy.38) | data formatting | bytes 524288 | tf_op jit(solution)/shard_map/while/body/eval_jaxpr/reshape | solution.py:31
  67.1 3.2 %select_add_fusion.2 = f32[512,1024]{1,0:T(8,128)S(1)} fusion(f32[512,1024]{1,0:T(8,128)S(1)} %copy-done, f32[512,128]{0,1:T(8,128)} %reshape.257, f32[128,1024]{1,0:T(8,128)S(1)} %reshape.259, pred[]{:T(512)S(6)} %compare.3), kind=kOutput, calls=%fused_computation.clone.1 | convolution fusion | flops 806354944 | bytes 4980737 | tf_op jit(solution)/shard_map/while/body/eval_jaxpr/dot_general | solution.py:53
  72.8 2.0 %broadcast_select_fusion.2 = s32[2]{0:T(128)} fusion(s32[2]{0:T(128)S(1)} %collective-permute-done.2, pred[]{:T(512)} %get-tuple-element.274, s32[1]{0:T(128)} %get-tuple-element.242, s32[1]{0:T(128)} %get-tuple-element.243), kind=kLoop, calls=%fused_computation.24.clone.1 | loop fusion | flops 4 | bytes 25 | tf_op jit(solution)/shard_map/while/body/eval_jaxpr/jit(_where)/select_n | solution.py:66
  75.9 1.9 %maximum_select_fusion.2 = f32[2,8,64,64]{3,2,1,0:T(8,128)} fusion(f32[2,8,64,64]{3,2,1,0:T(8,128)} %collective-permute-done, f32[1,8,64,64]{3,2,1,0:T(8,128)S(1)} %get-tuple-element.238, f32[1,8,64,64]{3,2,1,0:T(8,128)S(1)} %get-tuple-element.239, pred[]{:T(512)} %get-tuple-element.274), kind=kLoop, calls=%fused_computation.5.clone.1 | loop fusion | flops 131072 | bytes 786433 | tf_op jit(solution)/shard_map/while/body/eval_jaxpr/jit(_where)/select_n | solution.py:64
  93.3 2.2 %convolution_bitcast_fusion.6 = f32[8,64,2,64]{3,0,1,2:T(8,128)} fusion(f32[64,64,8]{1,0,2:T(8,128)} %dot_general.52, s32[8]{0:T(128)S(1)} %add_bitcast_fusion.6, s32[8,2]{0,1:T(2,128)} %multiply_add_fusion.6, pred[8]{0:T(512)(128)(4,1)S(1)} %iota_compare_fusion.6), kind=kOutput, calls=%fused_computation.2.clone.1 | convolution fusion | flops 6291712 | bytes 393320 | tf_op jit(solution)/shard_map/while/body/eval_jaxpr/dot_general | solution.py:22
  95.5 2.0 %copy.38 = f32[8,64,2,64]{1,0,3,2:T(8,128)} copy(f32[8,64,2,64]{3,0,1,2:T(8,128)} %convolution_bitcast_fusion.6) | data formatting | bytes 524288 | tf_op jit(solution)/shard_map/while/body/eval_jaxpr/transpose | solution.py:30
  99.4 3.2 %select_add_fusion.2 = f32[512,1024]{1,0:T(8,128)S(1)} fusion(f32[512,1024]{1,0:T(8,128)S(1)} %copy-done, f32[512,128]{0,1:T(8,128)} %reshape.257, f32[128,1024]{1,0:T(8,128)S(1)} %reshape.259, pred[]{:T(512)S(6)} %compare.3), kind=kOutput, calls=%fused_computation.clone.1 | convolution fusion | flops 806354944 | bytes 4980737 | tf_op jit(solution)/shard_map/while/body/eval_jaxpr/dot_general | solution.py:53
  104.7 2.0 %broadcast_select_fusion.2 = s32[2]{0:T(128)} fusion(s32[2]{0:T(128)S(1)} %collective-permute-done.2, pred[]{:T(512)} %get-tuple-element.274, s32[1]{0:T(128)} %get-tuple-element.242, s32[1]{0:T(128)} %get-tuple-element.243), kind=kLoop, calls=%fused_computation.24.clone.1 | loop fusion | flops 4 | bytes 25 | tf_op jit(solution)/shard_map/while/body/eval_jaxpr/jit(_where)/select_n | solution.py:66
  107.8 1.9 %maximum_select_fusion.2 = f32[2,8,64,64]{3,2,1,0:T(8,128)} fusion(f32[2,8,64,64]{3,2,1,0:T(8,128)} %collective-permute-done, f32[1,8,64,64]{3,2,1,0:T(8,128)S(1)} %get-tuple-element.238, f32[1,8,64,64]{3,2,1,0:T(8,128)S(1)} %get-tuple-element.239, pred[]{:T(512)} %get-tuple-element.274), kind=kLoop, calls=%fused_computation.5.clone.1 | loop fusion | flops 131072 | bytes 786433 | tf_op jit(solution)/shard_map/while/body/eval_jaxpr/jit(_where)/select_n | solution.py:64
  118.3 3.2 %convolution_add_fusion = f32[512,1024]{1,0:T(8,128)} fusion(f32[512,1024]{1,0:T(8,128)S(1)} %copy-done.2, f32[512,128]{0,1:T(8,128)S(1)} %reshape.240, f32[128,1024]{1,0:T(8,128)S(1)} %reshape.242), kind=kOutput, calls=%fused_computation.29 | convolution fusion | flops 805830656 | bytes 4980736 | tf_op jit(solution)/shard_map/dot_general | solution.py:53
  121.5 43.7 %reduce-scatter.2.cloned.1.call-done = f32[128,1024]{1,0:T(8,128)} async-done(((f32[512,1024]{1,0:T(8,128)}), f32[128,1024]{1,0:T(8,128)}) %reduce-scatter.2.cloned.1.call-update) | async-done | bytes 524304 | tf_op jit(solution)/shard_map/reduce_scatter | solution.py:75
  (140 shorter events, 61.7 us)
Async XLA Ops:
  6.5 158.7 %reduce-scatter.2.cloned.1.call-start = ((), (), s32[]{:S(2)}) async-start(), calls=%async_computation.1 | async-start | bytes 2621440 | tf_op jit(solution)/shard_map/reduce_scatter | solution.py:75
  12.9 30.8 %collective-permute-start = (f32[2,8,64,64]{3,2,1,0:T(8,128)}, f32[2,8,64,64]{3,2,1,0:T(8,128)}, u32[]{:S(2)}, u32[]{:S(2)}) collective-permute-start(f32[2,8,64,64]{3,2,1,0:T(8,128)} %get-tuple-element.257), channel_id=1, source_target_pairs={{4,0},{0,4},{5,1},{1,5},{6,2},{2,6},{7,3},{3,7},{12,8},{8,12},{13,... | collective-permute-start | bytes 786440 | tf_op jit(solution)/shard_map/while/body/eval_jaxpr/ppermute | solution.py:12
  15.9 27.7 %collective-permute-start.1 = (s32[2,8,2]{1,2,0:T(2,128)S(1)}, s32[2,8,2]{1,2,0:T(2,128)S(1)}, u32[]{:S(2)}, u32[]{:S(2)}) collective-permute-start(s32[2,8,2]{1,2,0:T(2,128)S(1)} %get-tuple-element.258), channel_id=1, source_target_pairs={{4,0},{0,4},{5,1},{1,5},{6,2},{2,6},{7,3},{3,7},{12,8},{8,12},{13,... | collective-permute-start | bytes 392 | tf_op jit(solution)/shard_map/while/body/eval_jaxpr/ppermute | solution.py:12
  16.0 23.6 %collective-permute-start.2 = (s32[2]{0:T(128)}, s32[2]{0:T(128)S(1)}, u32[]{:S(2)}, u32[]{:S(2)}) collective-permute-start(s32[2]{0:T(128)} %get-tuple-element.259), channel_id=1, source_target_pairs={{4,0},{0,4},{5,1},{1,5},{6,2},{2,6},{7,3},{3,7},{12,8},{8,12},{13,... | collective-permute-start | bytes 32 | tf_op jit(solution)/shard_map/while/body/eval_jaxpr/ppermute | solution.py:12
  19.1 27.6 %collective-permute-start.3 = (f32[24,64,64]{2,1,0:T(8,128)S(1)}, f32[24,64,64]{2,1,0:T(8,128)}, u32[]{:S(2)}, u32[]{:S(2)}) collective-permute-start(f32[24,64,64]{2,1,0:T(8,128)S(1)} %copy.52), channel_id=1, source_target_pairs={{8,0},{16,8},{24,16},{0,24},{9,1},{17,9},{25,17},{1,25},{10,2},{18... | collective-permute-start | bytes 1179656 | tf_op jit(solution)/shard_map/while/body/eval_jaxpr/ppermute | solution.py:12
  19.7 27.0 %collective-permute-start.4 = (s32[24,2]{0,1:T(2,128)}, s32[24,2]{0,1:T(2,128)S(1)}, u32[]{:S(2)}, u32[]{:S(2)}) collective-permute-start(s32[24,2]{0,1:T(2,128)} %copy.53), channel_id=1, source_target_pairs={{8,0},{16,8},{24,16},{0,24},{9,1},{17,9},{25,17},{1,25},{10,2},{18... | collective-permute-start | bytes 584 | tf_op jit(solution)/shard_map/while/body/eval_jaxpr/ppermute | solution.py:12
  26.8 9.6 %copy-start = (f32[512,1024]{1,0:T(8,128)S(1)}, f32[512,1024]{1,0:T(8,128)}, u32[]{:S(2)}) copy-start(f32[512,1024]{1,0:T(8,128)} %get-tuple-element.256) | copy-start | bytes 6291460 | tf_op jit(solution)/shard_map/while
  39.6 7.1 %copy-start.1 = (f32[512,1024]{1,0:T(8,128)}, f32[512,1024]{1,0:T(8,128)S(1)}, u32[]{:S(2)}) copy-start(f32[512,1024]{1,0:T(8,128)S(1)} %select_add_fusion.2) | copy-start | bytes 6291460 | tf_op jit(solution)/shard_map/while
  39.7 7.0 %collective-permute-start.5 = (s32[1]{0:T(128)}, s32[1]{0:T(128)}, u32[]{:S(2)}, u32[]{:S(2)}) collective-permute-start(s32[1]{0:T(128)} %copy.54), channel_id=1, source_target_pairs={{8,0},{16,8},{24,16},{0,24},{9,1},{17,9},{25,17},{1,25},{10,2},{18... | collective-permute-start | bytes 20 | tf_op jit(solution)/shard_map/while/body/eval_jaxpr/ppermute | solution.py:12
  47.4 27.5 %collective-permute-start = (f32[2,8,64,64]{3,2,1,0:T(8,128)}, f32[2,8,64,64]{3,2,1,0:T(8,128)}, u32[]{:S(2)}, u32[]{:S(2)}) collective-permute-start(f32[2,8,64,64]{3,2,1,0:T(8,128)} %get-tuple-element.257), channel_id=1, source_target_pairs={{4,0},{0,4},{5,1},{1,5},{6,2},{2,6},{7,3},{3,7},{12,8},{8,12},{13,... | collective-permute-start | bytes 786440 | tf_op jit(solution)/shard_map/while/body/eval_jaxpr/ppermute | solution.py:12
  47.4 27.4 %collective-permute-start.1 = (s32[2,8,2]{1,2,0:T(2,128)S(1)}, s32[2,8,2]{1,2,0:T(2,128)S(1)}, u32[]{:S(2)}, u32[]{:S(2)}) collective-permute-start(s32[2,8,2]{1,2,0:T(2,128)S(1)} %get-tuple-element.258), channel_id=1, source_target_pairs={{4,0},{0,4},{5,1},{1,5},{6,2},{2,6},{7,3},{3,7},{12,8},{8,12},{13,... | collective-permute-start | bytes 392 | tf_op jit(solution)/shard_map/while/body/eval_jaxpr/ppermute | solution.py:12
  49.5 20.9 %collective-permute-start.2 = (s32[2]{0:T(128)}, s32[2]{0:T(128)S(1)}, u32[]{:S(2)}, u32[]{:S(2)}) collective-permute-start(s32[2]{0:T(128)} %get-tuple-element.259), channel_id=1, source_target_pairs={{4,0},{0,4},{5,1},{1,5},{6,2},{2,6},{7,3},{3,7},{12,8},{8,12},{13,... | collective-permute-start | bytes 32 | tf_op jit(solution)/shard_map/while/body/eval_jaxpr/ppermute | solution.py:12
  50.7 27.2 %collective-permute-start.3 = (f32[24,64,64]{2,1,0:T(8,128)S(1)}, f32[24,64,64]{2,1,0:T(8,128)}, u32[]{:S(2)}, u32[]{:S(2)}) collective-permute-start(f32[24,64,64]{2,1,0:T(8,128)S(1)} %copy.52), channel_id=1, source_target_pairs={{8,0},{16,8},{24,16},{0,24},{9,1},{17,9},{25,17},{1,25},{10,2},{18... | collective-permute-start | bytes 1179656 | tf_op jit(solution)/shard_map/while/body/eval_jaxpr/ppermute | solution.py:12
  51.2 26.6 %collective-permute-start.4 = (s32[24,2]{0,1:T(2,128)}, s32[24,2]{0,1:T(2,128)S(1)}, u32[]{:S(2)}, u32[]{:S(2)}) collective-permute-start(s32[24,2]{0,1:T(2,128)} %copy.53), channel_id=1, source_target_pairs={{8,0},{16,8},{24,16},{0,24},{9,1},{17,9},{25,17},{1,25},{10,2},{18... | collective-permute-start | bytes 584 | tf_op jit(solution)/shard_map/while/body/eval_jaxpr/ppermute | solution.py:12
  57.5 9.6 %copy-start = (f32[512,1024]{1,0:T(8,128)S(1)}, f32[512,1024]{1,0:T(8,128)}, u32[]{:S(2)}) copy-start(f32[512,1024]{1,0:T(8,128)} %get-tuple-element.256) | copy-start | bytes 6291460 | tf_op jit(solution)/shard_map/while
  70.3 7.5 %copy-start.1 = (f32[512,1024]{1,0:T(8,128)}, f32[512,1024]{1,0:T(8,128)S(1)}, u32[]{:S(2)}) copy-start(f32[512,1024]{1,0:T(8,128)S(1)} %select_add_fusion.2) | copy-start | bytes 6291460 | tf_op jit(solution)/shard_map/while
  70.3 7.5 %collective-permute-start.5 = (s32[1]{0:T(128)}, s32[1]{0:T(128)}, u32[]{:S(2)}, u32[]{:S(2)}) collective-permute-start(s32[1]{0:T(128)} %copy.54), channel_id=1, source_target_pairs={{8,0},{16,8},{24,16},{0,24},{9,1},{17,9},{25,17},{1,25},{10,2},{18... | collective-permute-start | bytes 20 | tf_op jit(solution)/shard_map/while/body/eval_jaxpr/ppermute | solution.py:12
  78.5 28.2 %collective-permute-start = (f32[2,8,64,64]{3,2,1,0:T(8,128)}, f32[2,8,64,64]{3,2,1,0:T(8,128)}, u32[]{:S(2)}, u32[]{:S(2)}) collective-permute-start(f32[2,8,64,64]{3,2,1,0:T(8,128)} %get-tuple-element.257), channel_id=1, source_target_pairs={{4,0},{0,4},{5,1},{1,5},{6,2},{2,6},{7,3},{3,7},{12,8},{8,12},{13,... | collective-permute-start | bytes 786440 | tf_op jit(solution)/shard_map/while/body/eval_jaxpr/ppermute | solution.py:12
  79.2 27.5 %collective-permute-start.1 = (s32[2,8,2]{1,2,0:T(2,128)S(1)}, s32[2,8,2]{1,2,0:T(2,128)S(1)}, u32[]{:S(2)}, u32[]{:S(2)}) collective-permute-start(s32[2,8,2]{1,2,0:T(2,128)S(1)} %get-tuple-element.258), channel_id=1, source_target_pairs={{4,0},{0,4},{5,1},{1,5},{6,2},{2,6},{7,3},{3,7},{12,8},{8,12},{13,... | collective-permute-start | bytes 392 | tf_op jit(solution)/shard_map/while/body/eval_jaxpr/ppermute | solution.py:12
  80.6 22.0 %collective-permute-start.2 = (s32[2]{0:T(128)}, s32[2]{0:T(128)S(1)}, u32[]{:S(2)}, u32[]{:S(2)}) collective-permute-start(s32[2]{0:T(128)} %get-tuple-element.259), channel_id=1, source_target_pairs={{4,0},{0,4},{5,1},{1,5},{6,2},{2,6},{7,3},{3,7},{12,8},{8,12},{13,... | collective-permute-start | bytes 32 | tf_op jit(solution)/shard_map/while/body/eval_jaxpr/ppermute | solution.py:12
  82.4 27.3 %collective-permute-start.3 = (f32[24,64,64]{2,1,0:T(8,128)S(1)}, f32[24,64,64]{2,1,0:T(8,128)}, u32[]{:S(2)}, u32[]{:S(2)}) collective-permute-start(f32[24,64,64]{2,1,0:T(8,128)S(1)} %copy.52), channel_id=1, source_target_pairs={{8,0},{16,8},{24,16},{0,24},{9,1},{17,9},{25,17},{1,25},{10,2},{18... | collective-permute-start | bytes 1179656 | tf_op jit(solution)/shard_map/while/body/eval_jaxpr/ppermute | solution.py:12
  82.9 26.8 %collective-permute-start.4 = (s32[24,2]{0,1:T(2,128)}, s32[24,2]{0,1:T(2,128)S(1)}, u32[]{:S(2)}, u32[]{:S(2)}) collective-permute-start(s32[24,2]{0,1:T(2,128)} %copy.53), channel_id=1, source_target_pairs={{8,0},{16,8},{24,16},{0,24},{9,1},{17,9},{25,17},{1,25},{10,2},{18... | collective-permute-start | bytes 584 | tf_op jit(solution)/shard_map/while/body/eval_jaxpr/ppermute | solution.py:12
  89.8 9.6 %copy-start = (f32[512,1024]{1,0:T(8,128)S(1)}, f32[512,1024]{1,0:T(8,128)}, u32[]{:S(2)}) copy-start(f32[512,1024]{1,0:T(8,128)} %get-tuple-element.256) | copy-start | bytes 6291460 | tf_op jit(solution)/shard_map/while
  102.6 7.0 %collective-permute-start.5 = (s32[1]{0:T(128)}, s32[1]{0:T(128)}, u32[]{:S(2)}, u32[]{:S(2)}) collective-permute-start(s32[1]{0:T(128)} %copy.54), channel_id=1, source_target_pairs={{8,0},{16,8},{24,16},{0,24},{9,1},{17,9},{25,17},{1,25},{10,2},{18... | collective-permute-start | bytes 20 | tf_op jit(solution)/shard_map/while/body/eval_jaxpr/ppermute | solution.py:12
  (7 other events, 33.9 us)
Sparse Core Ops, SparseCore 0:
  121.7 43.5 reduce-scatter.1
where the time goes:
time: 174 us; the launch traced here: 172 us
  local copies, waits for them, and re-layouts  47.7 us (27%)
  waiting for transfers between devices  43.7 us (25%)
  matrix products  24.3 us (14%)
  other arithmetic  21.7 us (12%)
  starting transfers between devices  18.1 us (10%)
  between operations  14.2 us (8%)
  loops' own time  2.26 us (1%)
    reduce_scatter x1, waiting for transfers between devices, body(): lax.psum_scatter(partial_value, 'layer', scatter_dimension=0, tiled=True)  43.7 us
    ppermute x18, starting transfers between devices, from_behind(): return lax.ppermute(block, axis, route)  18.1 us
    dot_general x4, matrix products, product(): jnp.dot(left, right, precision=lax.Precision.HIGHEST, preferred_element_t...  12.8 us
    dot_general x8, matrix products, densify(): jnp.dot(select, values.reshape(slots, width * width), precision=lax.Preci...  11.5 us
    reshape x8, local copies, waits for them, and re-layouts, densify(): return flat.reshape(rows, cols, width, width).transpose(0, 2, 1, 3).resha...  8.16 us
    transpose x4, local copies, waits for them, and re-layouts, densify(): return flat.reshape(rows, cols, width, width).transpose(0, 2, 1, 3).resha...  7.12 us
    select_n x3, other arithmetic, advance(): an = jnp.where(last, jnp.roll(an, -1, 0), an)  6.05 us
    select_n x3, other arithmetic, advance(): av = jnp.where(last, jnp.roll(av, -1, 0), av)  5.76 us
  transfers between devices with their start and end apart: 19, of which 1 were waited for; matrix products, arithmetic and copies ran while one was open for 45% of the time, Pallas kernels for 0%

commit v1 on v0

v1 whole, which is shorter than its diff:
```python
import functools

import jax
import jax.numpy as jnp
from jax import lax
from jax.experimental import pallas as pl
from jax.experimental.pallas import tpu as pltpu
from jax.sharding import PartitionSpec as P

MESH = pl.DeviceIdType.MESH
TILE_ROWS = 8
CHUNKS = 4


def spread(inner, tile_cols, a_pos, a_num, b_pos, b_num, a_val, b_val, a_out, b_out, a_inv, b_inv):
    slots, caps, width = a_val.shape[0], a_val.shape[1], a_val.shape[2]
    for m in range(slots):
        for t in range(TILE_ROWS * inner):
            a_inv[m, t] = -1
        for s in range(caps):
            spot = a_pos[m, 2 * s] * inner + a_pos[m, 2 * s + 1]
            a_inv[m, spot] = jnp.where(s < a_num[m], s, a_inv[m, spot])
    for t in range(inner * tile_cols):
        b_inv[t] = -1
    for s in range(b_val.shape[0]):
        spot = b_pos[2 * s] * tile_cols + b_pos[2 * s + 1]
        b_inv[spot] = jnp.where(s < b_num[0], s, b_inv[spot])

    def block(ref, slot):
        value = ref[jnp.maximum(slot, 0)]
        return jnp.where(slot >= 0, value, jnp.zeros_like(value))

    for m in range(slots):
        for r in range(TILE_ROWS):
            pair = [block(a_val.at[m], a_inv[m, r * inner + c]) for c in range(inner)]
            a_out[pl.ds(r * width, width), pl.ds(m * inner * width, inner * width)] = jnp.concatenate(pair, 1)
    for r in range(inner):
        for c in range(0, tile_cols, 2):
            pair = [block(b_val, b_inv[r * tile_cols + c + d]) for d in range(2)]
            b_out[pl.ds(r * width, width), pl.ds(c * width, 2 * width)] = jnp.concatenate(pair, 1)


def halves(x):
    high = x.astype(jnp.bfloat16)
    return high, (x - high.astype(jnp.float32)).astype(jnp.bfloat16)


def dot(x, y):
    xh, xl = halves(x)
    yh, yl = halves(y)
    f = functools.partial(jnp.dot, preferred_element_type=jnp.float32)
    return f(xh, yh) + (f(xh, yl) + f(xl, yh))


def powers(n):
    out, b = [], n // 2
    while b:
        out.append(b)
        b //= 2
    return out


def multiply(rows, cols, part, depth, n_copies, a_ref, b_ref, out_ref, a_full, b_full, sent, landed, send_sem, recv_sem, local_sem):
    i, j, l = lax.axis_index("row"), lax.axis_index("col"), lax.axis_index("layer")
    row_bits, col_bits = powers(rows), powers(cols)
    slots = rows // cols
    width = b_ref.shape[1] // CHUNKS
    partner = l + 1 - 2 * (l % 2)
    is_inner = jnp.logical_or(l == 1, l == 2)
    is_outer = jnp.logical_or(l == 0, l == 3)
    inner_dest = 1 + l // 2
    outer_dest = 3 * (l // 2)
    far_lo = pl.multiple_of(2 * part * (1 - l // 2), 2 * part)
    near_lo = pl.multiple_of(2 * part * (l // 2), 2 * part)
    inner_lo = pl.multiple_of(part * inner_dest, part)
    outer_lo = pl.multiple_of(part * outer_dest, part)

    def flip(x, bit):
        return x + bit - 2 * bit * ((x // bit) % 2)

    ids = iter(range(n_copies))
    pending = []

    def copy(src, dst, device, back=0):
        k = next(ids)
        return pltpu.make_async_remote_copy(
            src_ref=src, dst_ref=dst, send_sem=send_sem.at[k], recv_sem=recv_sem.at[k - back],
            device_id=device, device_id_type=MESH)

    def when(cond, act):
        if cond is None:
            act()
        else:
            pl.when(cond)(act)

    def start(copies, cond=None):
        when(cond, lambda: [c.start() for c in copies] and None)
        pending.append((copies, cond))

    def arrive(copies, cond=None):
        when(cond, lambda: [c.wait_recv() for c in copies] and None)

    def depart(entry):
        copies, cond = entry
        when(cond, lambda: [c.wait_send() for c in copies] and None)

    def at(piece):
        return pl.ds(pl.multiple_of(piece * depth, depth), depth)

    def b_view(q, piece, c):
        return b_full.at[q, at(piece), pl.ds(c * width, width)]

    def b_stage(q, c, stage):
        bit = row_bits[stage]
        offsets = [0]
        for b in row_bits[:stage]:
            offsets = offsets + [o + b for o in offsets]
        copies = []
        for o in offsets:
            owner = i
            for b in row_bits[:stage]:
                if o & b:
                    owner = flip(owner, b)
            piece = (owner + j) % rows
            if q == 0 and o == 0:
                src = b_ref.at[:, pl.ds(c * width, width)]
            else:
                src = b_view(q, piece, c)
            copies.append(copy(src, b_view(q, piece, c), {"row": flip(i, bit)}))
        return copies

    def a_view(q, lo, size, piece):
        return a_full.at[q, pl.ds(lo, size), at(piece)]

    def a_stage(q, lo, size, stage):
        bit = col_bits[stage]
        owners = [j]
        for b in col_bits[:stage]:
            owners = owners + [flip(o, b) for o in owners]
        copies = []
        for n, o in enumerate(owners):
            for m in range(slots):
                piece = (i + o + cols * m) % rows
                if q == 0 and n == 0:
                    src = a_ref.at[pl.ds(lo, size), pl.ds(m * depth, depth)]
                else:
                    src = a_view(q, lo, size, piece)
                copies.append(copy(src, a_view(q, lo, size, piece), {"col": flip(j, bit)}))
        return copies

    my_pieces = [(i + j + cols * m) % rows for m in range(slots)]
    to_partner = {"layer": partner}

    def z_a(lo, size):
        return [copy(a_ref.at[pl.ds(lo, size), pl.ds(m * depth, depth)],
                     a_view(1, lo, size, my_pieces[m]), to_partner) for m in range(slots)]

    def z_b(c):
        return [copy(b_ref.at[:, pl.ds(c * width, width)], b_view(1, my_pieces[0], c), to_partner)]

    barrier = pltpu.get_barrier_semaphore()
    peers = [{"row": flip(i, b)} for b in row_bits] + [{"col": flip(j, b)} for b in col_bits]
    peers += [{"layer": (l + d) % 4} for d in (1, 2, 3)]
    for peer in peers:
        pl.semaphore_signal(barrier, inc=1, device_id=peer, device_id_type=MESH)
    pl.semaphore_wait(barrier, len(peers))

    def a_finish(q, lo, size, first, cond):
        arrive(first, cond)
        for stage in range(1, len(col_bits)):
            more = a_stage(q, lo, size, stage)
            start(more, cond)
            arrive(more, cond)

    def b_relay(q, c, first, cond):
        arrive(first, cond)
        for stage in range(1, len(row_bits)):
            more = b_stage(q, c, stage)
            start(more, cond)
            if stage < len(row_bits) - 1:
                arrive(more, cond)
        return more

    za_far, zb = z_a(far_lo, 2 * part), [z_b(c) for c in range(CHUNKS)]
    za_inner = z_a(inner_lo, part)
    start(za_far, is_outer)
    far0 = a_stage(0, far_lo, 2 * part, 0)
    start(far0, is_inner)
    b0 = [None] * CHUNKS
    b1 = [None] * CHUNKS
    b0[0] = b_stage(0, 0, 0)
    start(b0[0])
    start(zb[0], is_outer)
    own = [pltpu.make_async_copy(b_ref, b_full.at[0, at(my_pieces[0])], local_sem.at[0])]
    for m in range(slots):
        own.append(pltpu.make_async_copy(
            a_ref.at[:, pl.ds(m * depth, depth)], a_full.at[0, :, at(my_pieces[m])], local_sem.at[1 + m]))
    for c in own:
        c.start()
    near0 = a_stage(0, near_lo, 2 * part, 0)
    start(near0, is_outer)
    last0 = [None] * CHUNKS
    last1 = [None] * CHUNKS
    last0[0] = b_relay(0, 0, b0[0], None)
    b0[1] = b_stage(0, 1, 0)
    arrive(za_far, is_inner)
    far1 = a_stage(1, far_lo, 2 * part, 0)
    start(far1, is_inner)
    arrive(zb[0], is_inner)
    b1[0] = b_stage(1, 0, 0)
    start(b1[0], is_inner)
    start(b0[1])
    depart((za_far, is_outer))
    pending.remove((za_far, is_outer))
    start(zb[1], is_outer)
    last1[0] = b_relay(1, 0, b1[0], is_inner)
    for c in own:
        c.wait()
    a_finish(0, far_lo, 2 * part, far0, is_inner)
    a_finish(1, far_lo, 2 * part, far1, is_inner)
    start(near0, is_inner)

    step = min(rows * depth, 512)

    def product(q, lo, size, c):
        total = rows * depth // step

        def term(k):
            at_k = pl.ds(pl.multiple_of(k * step, step), step)
            return dot(a_full[q, pl.ds(lo, size), at_k], b_full[q, at_k, pl.ds(c * width, width)])

        if total == 1:
            return term(0)
        return lax.fori_loop(0, total, lambda k, s: s + term(k), jnp.zeros((size, width), jnp.float32))

    def chunk(c):
        return pl.ds(c * width, width)

    results = []

    def far_chunk(c):
        def act():
            value = product(0, far_lo, 2 * part, c) + product(1, far_lo, 2 * part, c)
            sent[0, :, chunk(c)] = value[:part]
            sent[1, :, chunk(c)] = value[part:]
        when(is_inner, act)
        first = 2 * (1 - l // 2)
        copies = []
        for n in range(2):
            copies.append(copy(sent.at[n, :, chunk(c)], landed.at[0, :, chunk(c)], {"layer": first + n}, n))
        start(copies, is_inner)
        return copies[0]

    def near_chunk(c):
        def act():
            sent[2, :, chunk(c)] = product(0, outer_lo, part, c)
        when(is_inner, act)
        copies = [copy(sent.at[2, :, chunk(c)], landed.at[1, :, chunk(c)], to_partner)]
        start(copies, is_inner)
        return copies[0]

    def outer_chunk(c):
        def act():
            out_ref[:, chunk(c)] = product(0, outer_lo, part, c)
        when(is_outer, act)

    def inner_chunk(c):
        def act():
            out_ref[:, chunk(c)] = product(0, inner_lo, part, c) + product(1, inner_lo, part, c)
        when(is_inner, act)

    far_sent, near_sent = [None] * CHUNKS, [None] * CHUNKS
    for c in range(CHUNKS):
        if c + 1 < CHUNKS:
            arrive(zb[c + 1], is_inner)
            b1[c + 1] = b_stage(1, c + 1, 0)
            start(b1[c + 1], is_inner)
            if c + 2 < CHUNKS:
                b0[c + 2] = b_stage(0, c + 2, 0)
                start(b0[c + 2])
                start(zb[c + 2], is_outer)
            else:
                start(za_inner, is_outer)
        arrive(last0[c])
        arrive(last1[c], is_inner)
        far_sent[c] = far_chunk(c)
        if c + 1 < CHUNKS:
            last0[c + 1] = b_relay(0, c + 1, b0[c + 1], None)
            last1[c + 1] = b_relay(1, c + 1, b1[c + 1], is_inner)
        if c == 0:
            a_finish(0, near_lo, 2 * part, near0, None)
        else:
            near_sent[c - 1] = near_chunk(c - 1)
        outer_chunk(c)
    near_sent[CHUNKS - 1] = near_chunk(CHUNKS - 1)
    arrive(za_inner, is_inner)
    inner1 = a_stage(1, inner_lo, part, 0)
    start(inner1, is_inner)
    a_finish(1, inner_lo, part, inner1, is_inner)
    for c in range(CHUNKS):
        inner_chunk(c)
        far_sent[c].wait_recv()
        out_ref[:, chunk(c)] += landed[0, :, chunk(c)]

        def add(c=c):
            near_sent[c].wait_recv()
            out_ref[:, chunk(c)] += landed[1, :, chunk(c)]
        when(is_outer, add)
    for entry in pending:
        depart(entry)


def body(rows, cols, a_values, a_places, a_counts, b_values, b_places, b_counts):
    a_vals = a_values.reshape(a_values.shape[3:])
    b_vals = b_values.reshape(b_values.shape[3:])
    slots, cap, width = a_vals.shape[:3]
    layers = lax.axis_size("layer")
    inner = TILE_ROWS // layers
    tile_cols = TILE_ROWS * rows // cols
    a_pos = a_places.reshape(slots, 2 * cap)
    a_num = a_counts.reshape(slots)
    b_pos = b_places.reshape(2 * b_vals.shape[0])
    b_num = b_counts.reshape(1)
    depth, part = inner * width, TILE_ROWS * width // layers
    full_rows, full_cols = TILE_ROWS * width, tile_cols * width
    f32 = jnp.float32
    vmem = pl.BlockSpec(memory_space=pltpu.VMEM)
    smem = pl.BlockSpec(memory_space=pltpu.SMEM)
    a_dense, b_dense = pl.pallas_call(
        functools.partial(spread, inner, tile_cols),
        out_shape=(jax.ShapeDtypeStruct((full_rows, slots * depth), f32), jax.ShapeDtypeStruct((depth, full_cols), f32)),
        in_specs=[smem] * 4 + [vmem] * 2,
        out_specs=(vmem, vmem),
        scratch_shapes=[pltpu.SMEM((slots, TILE_ROWS * inner), jnp.int32), pltpu.SMEM((inner * tile_cols,), jnp.int32)],
    )(a_pos, a_num, b_pos, b_num, a_vals, b_vals)

    n_copies = 2 * CHUNKS * (rows - 1) + 4 * slots * (cols - 1) + 2 * slots + CHUNKS * 4
    return pl.pallas_call(
        functools.partial(multiply, rows, cols, part, depth, n_copies),
        out_shape=jax.ShapeDtypeStruct((part, full_cols), f32),
        in_specs=[vmem, vmem],
        out_specs=vmem,
        scratch_shapes=[
            pltpu.VMEM((2, full_rows, rows * depth), f32),
            pltpu.VMEM((2, rows * depth, full_cols), f32),
            pltpu.VMEM((3, part, full_cols), f32),
            pltpu.VMEM((2, part, full_cols), f32),
            pltpu.SemaphoreType.DMA((n_copies,)),
            pltpu.SemaphoreType.DMA((n_copies,)),
            pltpu.SemaphoreType.DMA((1 + slots,)),
        ],
        compiler_params=pltpu.CompilerParams(collective_id=0, has_side_effects=True, vmem_limit_bytes=48 * 2**20),
    )(a_dense, b_dense)


def solution(mesh):
    in_specs = (
        P("row", "col", "layer", None, None, None, None),
        P("row", "col", "layer", None, None, None),
        P("row", "col", "layer", None),
        P("row", "col", "layer", None, None, None),
        P("row", "col", "layer", None, None),
        P("row", "col", "layer"),
    )
    out_specs = P(("row", "layer"), "col")
    call = functools.partial(body, mesh.shape["row"], mesh.shape["col"])
    return jax.shard_map(call, mesh=mesh, in_specs=in_specs, out_specs=out_specs, check_vma=False)
```

time: 174 us -> 60.7 us (0.35)
  Pallas kernels: 0 us -> 54.6 us
  waiting for transfers between devices: 43.7 us -> 0 us
  local copies, waits for them, and re-layouts: 47.7 us -> 5.08 us
  matrix products: 24.3 us -> 0 us
  other arithmetic: 21.7 us -> 0 us
  starting transfers between devices: 18.1 us -> 0 us
  between operations: 14.2 us -> 0.67 us
  loops' own time: 2.26 us -> 0 us
    pallas_call x0 -> x2, Pallas kernels: none -> 54.6 us  [the longest x1 51.9 us: body(): pl.pallas_call(functools.partial(multiply, rows, cols, part, depth, n_cop...]
    reduce_scatter x1 -> x0, waiting for transfers between devices: 43.7 us -> none  [body(): lax.psum_scatter(partial_value, 'layer', scatter_dimension=0, tiled=True)]
    dot_general x12 -> x0, matrix products: 24.3 us -> none  [the longest x4 12.8 us: product(): jnp.dot(left, right, precision=lax.Precision.HIGHEST, preferred_element_t...]
    ppermute x18 -> x0, starting transfers between devices: 18.1 us -> none  [from_behind(): return lax.ppermute(block, axis, route)]
    select_n x9 -> x0, other arithmetic: 11.8 us -> none  [the longest x3 6.05 us: advance(): an = jnp.where(last, jnp.roll(an, -1, 0), an)]
    slice x13 -> x0, local copies, waits for them, and re-layouts: 11.3 us -> none  [the longest x3 5 us: advance(): partial_value = partial_value + product(av[0], ap[0], an[0], bv, bp, bn[0])]
    reshape x12 -> x2, local copies, waits for them, and re-layouts: 10.4 us -> 1.33 us  [the longest x1 0.68 us: body(): b_pos = b_places.reshape(2 * b_vals.shape[0])]
    transpose x4 -> x0, local copies, waits for them, and re-layouts: 7.12 us -> none  [densify(): return flat.reshape(rows, cols, width, width).transpose(0, 2, 1, 3).resha...]
  transfers between devices with their start and end apart: 19 -> 0, of which waited for: 1 -> 0; matrix products, arithmetic and copies ran while one was open for 45% -> 0% of each run, Pallas kernels for 0% -> 0%
where the time goes in v1:
time: 60.7 us; the launch traced here: 60.4 us
  Pallas kernels  54.6 us (90%)
  local copies, waits for them, and re-layouts  5.08 us (8%)
  between operations  0.67 us (1%)
    pallas_call x1, Pallas kernels, body(): pl.pallas_call(functools.partial(multiply, rows, cols, part, depth, n_cop...  51.9 us
    unnamed x11, local copies, waits for them, and re-layouts  3.75 us
    pallas_call x1, Pallas kernels, body(): pl.pallas_call(functools.partial(spread, inner, tile_cols), out_shape=(ja...  2.7 us

profile of v1, /device:TPU:0, one launch (start us, length us, event | category | flops | bytes accessed | tf_op | source)
XLA Modules:
  0.0 60.4 jit_solution(1567113614991592818)
XLA Ops:
  0.7 0.0 copy-start.2
  0.7 0.7 %copy-done.2 = s32[1,1,1,2,8,2]{4,5,3,2,1,0:T(2,128)S(1)} copy-done((s32[1,1,1,2,8,2]{4,5,3,2,1,0:T(2,128)S(1)}, s32[1,1,1,2,8,2]{4,5,3,2,1,0:T(2,128)}, u32[]{:S(2)}) %copy-start.2) | copy-done | bytes 152
  1.3 0.1 copy.9
  1.4 0.0 copy-start.3
  1.4 0.7 %reshape.18.a_pos = s32[2,16]{1,0:T(2,128)} reshape(s32[1,1,1,2,8,2]{5,4,3,2,1,0:T(8,128)S(1)} %copy.9) | data formatting | bytes 256 | tf_op jit(solution)/shard_map/reshape | solution.py:320
  2.1 0.0 copy-done.3
  2.1 0.1 copy.10
  2.2 0.7 %reshape.20.b_pos = s32[48]{0:T(128)} reshape(s32[1,1,1,24,2]{4,3,2,1,0:T(8,128)S(1)} %copy.10) | data formatting | bytes 384 | tf_op jit(solution)/shard_map/reshape | solution.py:322
  2.9 2.7 %shard_map.64 = (f32[512,256]{1,0:T(8,128)}, f32[128,1024]{1,0:T(8,128)}) custom-call(s32[2,16]{1,0:T(2,128)} %reshape.18.a_pos, s32[2]{0:T(128)} %bitcast.11, s32[48]{0:T(128)} %reshape.20.b_pos, s32[1]{0:T(128)} %bitcast.8.b_num, f32[2,8,64,64]{3,2,1,0:T(8,128)} %bitcast.10, f32[24,64,64]{2,1,0:T(8,128)} %bitcast.9), custom_call_target="tpu_custom_call" | custom-call | tf_op jit(solution)/shard_map/pallas_call | solution.py:329
  5.6 0.0 copy-start
  5.6 1.0 %copy-done = f32[512,256]{1,0:T(8,128)S(1)} copy-done((f32[512,256]{1,0:T(8,128)S(1)}, f32[512,256]{1,0:T(8,128)}, u32[]{:S(2)}) %copy-start) | copy-done | bytes 524312
  6.6 0.0 copy-start.1
  6.6 1.0 %copy-done.1 = f32[128,1024]{1,0:T(8,128)S(1)} copy-done((f32[128,1024]{1,0:T(8,128)S(1)}, f32[128,1024]{1,0:T(8,128)}, u32[]{:S(2)}) %copy-start.1) | copy-done | bytes 524312
  7.6 51.9 %shard_map.65 = f32[128,1024]{1,0:T(8,128)S(1)} custom-call(f32[512,256]{1,0:T(8,128)S(1)} %copy-done, f32[128,1024]{1,0:T(8,128)S(1)} %copy-done.1), custom_call_target="tpu_custom_call" | custom-call | tf_op jit(solution)/shard_map/pallas_call | solution.py:338
  59.6 0.8 %copy.13 = f32[128,1024]{1,0:T(8,128)} copy(f32[128,1024]{1,0:T(8,128)S(1)} %shard_map.65) | data formatting | bytes 1048576
Async XLA Ops:
  0.7 0.7 %copy-start.2 = (s32[1,1,1,2,8,2]{4,5,3,2,1,0:T(2,128)S(1)}, s32[1,1,1,2,8,2]{4,5,3,2,1,0:T(2,128)}, u32[]{:S(2)}) copy-start(s32[1,1,1,2,8,2]{4,5,3,2,1,0:T(2,128)} %param.7) | copy-start | bytes 388
  1.4 0.7 %copy-start.3 = (s32[1,1,1,24,2]{3,4,2,1,0:T(2,128)S(1)}, s32[1,1,1,24,2]{3,4,2,1,0:T(2,128)}, u32[]{:S(2)}) copy-start(s32[1,1,1,24,2]{3,4,2,1,0:T(2,128)} %param.10) | copy-start | bytes 580
  5.6 1.0 %copy-start = (f32[512,256]{1,0:T(8,128)S(1)}, f32[512,256]{1,0:T(8,128)}, u32[]{:S(2)}) copy-start(f32[512,256]{1,0:T(8,128)} %get-tuple-element.7.a_ref) | copy-start | bytes 1572868
  6.6 1.0 %copy-start.1 = (f32[128,1024]{1,0:T(8,128)S(1)}, f32[128,1024]{1,0:T(8,128)}, u32[]{:S(2)}) copy-start(f32[128,1024]{1,0:T(8,128)} %get-tuple-element.8.b_ref) | copy-start | bytes 1572868

commit v2 on v1

--- a/solution.py
+++ b/solution.py
@@ -12,32 +12,15 @@
 CHUNKS = 4
 
 
-def spread(inner, tile_cols, a_pos, a_num, b_pos, b_num, a_val, b_val, a_out, b_out, a_inv, b_inv):
-    slots, caps, width = a_val.shape[0], a_val.shape[1], a_val.shape[2]
-    for m in range(slots):
-        for t in range(TILE_ROWS * inner):
-            a_inv[m, t] = -1
-        for s in range(caps):
-            spot = a_pos[m, 2 * s] * inner + a_pos[m, 2 * s + 1]
-            a_inv[m, spot] = jnp.where(s < a_num[m], s, a_inv[m, spot])
-    for t in range(inner * tile_cols):
-        b_inv[t] = -1
-    for s in range(b_val.shape[0]):
-        spot = b_pos[2 * s] * tile_cols + b_pos[2 * s + 1]
-        b_inv[spot] = jnp.where(s < b_num[0], s, b_inv[spot])
-
-    def block(ref, slot):
-        value = ref[jnp.maximum(slot, 0)]
-        return jnp.where(slot >= 0, value, jnp.zeros_like(value))
-
-    for m in range(slots):
-        for r in range(TILE_ROWS):
-            pair = [block(a_val.at[m], a_inv[m, r * inner + c]) for c in range(inner)]
-            a_out[pl.ds(r * width, width), pl.ds(m * inner * width, inner * width)] = jnp.concatenate(pair, 1)
-    for r in range(inner):
-        for c in range(0, tile_cols, 2):
-            pair = [block(b_val, b_inv[r * tile_cols + c + d]) for d in range(2)]
-            b_out[pl.ds(r * width, width), pl.ds(c * width, 2 * width)] = jnp.concatenate(pair, 1)
+def inverse(spots, total, bits):
+    each = 32 // bits
+    words = [jnp.int32(0)] * (-(-total // each))
+    for s, spot in enumerate(spots):
+        mark = jnp.left_shift(jnp.int32(s + 1), bits * (spot % each))
+        for w in range(len(words)):
+            inside = jnp.logical_and(spot >= w * each, spot < (w + 1) * each)
+            words[w] = words[w] + jnp.where(inside, mark, 0)
+    return [jnp.right_shift(words[t // each], bits * (t % each)) & (2**bits - 1) for t in range(total)]
 
 
 def halves(x):
@@ -60,11 +43,14 @@
     return out
 
 
-def multiply(rows, cols, part, depth, n_copies, a_ref, b_ref, out_ref, a_full, b_full, sent, landed, send_sem, recv_sem, local_sem):
+def multiply(rows, cols, part, depth, n_copies, *refs):
+    hbm, out_ref, held = refs[:6], refs[6], refs[7:13]
+    a_pos, a_num, b_pos, b_num, a_val, b_val = held
+    a_full, b_full, sent, landed, send_sem, recv_sem, local_sem = refs[13:]
     i, j, l = lax.axis_index("row"), lax.axis_index("col"), lax.axis_index("layer")
     row_bits, col_bits = powers(rows), powers(cols)
     slots = rows // cols
-    width = b_ref.shape[1] // CHUNKS
+    width = b_full.shape[2] // CHUNKS
     partner = l + 1 - 2 * (l % 2)
     is_inner = jnp.logical_or(l == 1, l == 2)
     is_outer = jnp.logical_or(l == 0, l == 3)
@@ -122,10 +108,7 @@
                 if o & b:
                     owner = flip(owner, b)
             piece = (owner + j) % rows
-            if q == 0 and o == 0:
-                src = b_ref.at[:, pl.ds(c * width, width)]
-            else:
-                src = b_view(q, piece, c)
+            src = b_view(q, piece, c)
             copies.append(copy(src, b_view(q, piece, c), {"row": flip(i, bit)}))
         return copies
 
@@ -138,13 +121,10 @@
         for b in col_bits[:stage]:
             owners = owners + [flip(o, b) for o in owners]
         copies = []
-        for n, o in enumerate(owners):
+        for o in owners:
             for m in range(slots):
                 piece = (i + o + cols * m) % rows
-                if q == 0 and n == 0:
-                    src = a_ref.at[pl.ds(lo, size), pl.ds(m * depth, depth)]
-                else:
-                    src = a_view(q, lo, size, piece)
+                src = a_view(q, lo, size, piece)
                 copies.append(copy(src, a_view(q, lo, size, piece), {"col": flip(j, bit)}))
         return copies
 
@@ -152,17 +132,58 @@
     to_partner = {"layer": partner}
 
     def z_a(lo, size):
-        return [copy(a_ref.at[pl.ds(lo, size), pl.ds(m * depth, depth)],
+        return [copy(a_view(0, lo, size, my_pieces[m]),
                      a_view(1, lo, size, my_pieces[m]), to_partner) for m in range(slots)]
 
     def z_b(c):
-        return [copy(b_ref.at[:, pl.ds(c * width, width)], b_view(1, my_pieces[0], c), to_partner)]
+        return [copy(b_view(0, my_pieces[0], c), b_view(1, my_pieces[0], c), to_partner)]
+
+    loads = [pltpu.make_async_copy(src, dst, local_sem.at[n]) for n, (src, dst) in enumerate(zip(hbm, held))]
+    for load in loads:
+        load.start()
 
     barrier = pltpu.get_barrier_semaphore()
     peers = [{"row": flip(i, b)} for b in row_bits] + [{"col": flip(j, b)} for b in col_bits]
     peers += [{"layer": (l + d) % 4} for d in (1, 2, 3)]
     for peer in peers:
         pl.semaphore_signal(barrier, inc=1, device_id=peer, device_id_type=MESH)
+
+    for load in loads[:4]:
+        load.wait()
+
+    block = a_val.shape[-1]
+    inner, tile_cols = depth // block, b_full.shape[2] // block
+    caps = a_val.shape[1]
+    a_slot = [
+        inverse([jnp.where(s < a_num[m], a_pos[m, 0, s] * inner + a_pos[m, 1, s], -1) for s in range(caps)],
+                TILE_ROWS * inner, 4)
+        for m in range(slots)
+    ]
+    b_slot = inverse(
+        [jnp.where(s < b_num[0], b_pos[0, s] * tile_cols + b_pos[1, s], -1) for s in range(b_val.shape[0])],
+        inner * tile_cols, 8)
+
+    def stored(ref, slot):
+        value = ref[jnp.maximum(slot - 1, 0)]
+        return jnp.where(slot > 0, value, jnp.zeros_like(value))
+
+    def a_dense():
+        for m in range(slots):
+            for r in range(TILE_ROWS):
+                parts = [stored(a_val.at[m], a_slot[m][r * inner + k]) for k in range(inner)]
+                a_full[0, pl.ds(r * block, block), at(my_pieces[m])] = jnp.concatenate(parts, 1)
+
+    def b_dense(c):
+        for r in range(inner):
+            rows_r = pl.ds(pl.multiple_of(my_pieces[0] * depth + r * block, block), block)
+            for k in range(c * width // block, (c + 1) * width // block, 2):
+                parts = [stored(b_val, b_slot[r * tile_cols + k + d]) for d in range(2)]
+                b_full[0, rows_r, pl.ds(k * block, 2 * block)] = jnp.concatenate(parts, 1)
+
+    for load in loads[4:]:
+        load.wait()
+    a_dense()
+    b_dense(0)
     pl.semaphore_wait(barrier, len(peers))
 
     def a_finish(q, lo, size, first, cond):
@@ -191,12 +212,8 @@
     b0[0] = b_stage(0, 0, 0)
     start(b0[0])
     start(zb[0], is_outer)
-    own = [pltpu.make_async_copy(b_ref, b_full.at[0, at(my_pieces[0])], local_sem.at[0])]
-    for m in range(slots):
-        own.append(pltpu.make_async_copy(
-            a_ref.at[:, pl.ds(m * depth, depth)], a_full.at[0, :, at(my_pieces[m])], local_sem.at[1 + m]))
-    for c in own:
-        c.start()
+    for c in range(1, CHUNKS):
+        b_dense(c)
     near0 = a_stage(0, near_lo, 2 * part, 0)
     start(near0, is_outer)
     last0 = [None] * CHUNKS
@@ -214,8 +231,6 @@
     pending.remove((za_far, is_outer))
     start(zb[1], is_outer)
     last1[0] = b_relay(1, 0, b1[0], is_inner)
-    for c in own:
-        c.wait()
     a_finish(0, far_lo, 2 * part, far0, is_inner)
     a_finish(1, far_lo, 2 * part, far1, is_inner)
     start(near0, is_inner)
@@ -313,44 +328,38 @@
 def body(rows, cols, a_values, a_places, a_counts, b_values, b_places, b_counts):
     a_vals = a_values.reshape(a_values.shape[3:])
     b_vals = b_values.reshape(b_values.shape[3:])
-    slots, cap, width = a_vals.shape[:3]
+    slots, width = a_vals.shape[0], a_vals.shape[2]
     layers = lax.axis_size("layer")
     inner = TILE_ROWS // layers
     tile_cols = TILE_ROWS * rows // cols
-    a_pos = a_places.reshape(slots, 2 * cap)
+    a_pos = jnp.swapaxes(a_places.reshape(a_places.shape[3:]), 1, 2)
     a_num = a_counts.reshape(slots)
-    b_pos = b_places.reshape(2 * b_vals.shape[0])
+    b_pos = b_places.reshape(b_places.shape[3:]).T
     b_num = b_counts.reshape(1)
     depth, part = inner * width, TILE_ROWS * width // layers
     full_rows, full_cols = TILE_ROWS * width, tile_cols * width
     f32 = jnp.float32
     vmem = pl.BlockSpec(memory_space=pltpu.VMEM)
-    smem = pl.BlockSpec(memory_space=pltpu.SMEM)
-    a_dense, b_dense = pl.pallas_call(
-        functools.partial(spread, inner, tile_cols),
-        out_shape=(jax.ShapeDtypeStruct((full_rows, slots * depth), f32), jax.ShapeDtypeStruct((depth, full_cols), f32)),
-        in_specs=[smem] * 4 + [vmem] * 2,
-        out_specs=(vmem, vmem),
-        scratch_shapes=[pltpu.SMEM((slots, TILE_ROWS * inner), jnp.int32), pltpu.SMEM((inner * tile_cols,), jnp.int32)],
-    )(a_pos, a_num, b_pos, b_num, a_vals, b_vals)
-
     n_copies = 2 * CHUNKS * (rows - 1) + 4 * slots * (cols - 1) + 2 * slots + CHUNKS * 4
     return pl.pallas_call(
         functools.partial(multiply, rows, cols, part, depth, n_copies),
         out_shape=jax.ShapeDtypeStruct((part, full_cols), f32),
-        in_specs=[vmem, vmem],
+        in_specs=[pl.BlockSpec(memory_space=pltpu.HBM)] * 6,
         out_specs=vmem,
         scratch_shapes=[
+            *[pltpu.SMEM(x.shape, jnp.int32) for x in (a_pos, a_num, b_pos, b_num)],
+            pltpu.VMEM(a_vals.shape, f32),
+            pltpu.VMEM(b_vals.shape, f32),
             pltpu.VMEM((2, full_rows, rows * depth), f32),
             pltpu.VMEM((2, rows * depth, full_cols), f32),
             pltpu.VMEM((3, part, full_cols), f32),
             pltpu.VMEM((2, part, full_cols), f32),
             pltpu.SemaphoreType.DMA((n_copies,)),
             pltpu.SemaphoreType.DMA((n_copies,)),
-            pltpu.SemaphoreType.DMA((1 + slots,)),
+            pltpu.SemaphoreType.DMA((6,)),
         ],
-        compiler_params=pltpu.CompilerParams(collective_id=0, has_side_effects=True, vmem_limit_bytes=48 * 2**20),
-    )(a_dense, b_dense)
+        compiler_params=pltpu.CompilerParams(collective_id=0, has_side_effects=True, vmem_limit_bytes=63 * 2**20),
+    )(a_pos, a_num, b_pos, b_num, a_vals, b_vals)
 
 
 def solution(mesh):

time: 60.7 us -> 55.6 us (0.916)
  local copies, waits for them, and re-layouts: 5.08 us -> 1.89 us
  Pallas kernels: 54.6 us -> 52.9 us
    pallas_call x1 -> x0, Pallas kernels: 2.7 us -> none  [body(): pl.pallas_call(functools.partial(spread, inner, tile_cols), out_shape=(ja...]
    unnamed x11 -> x1, local copies, waits for them, and re-layouts: 3.75 us -> 1.89 us
    reshape x2 -> x0, local copies, waits for them, and re-layouts: 1.33 us -> none  [the longest x1 0.68 us: body(): b_pos = b_places.reshape(2 * b_vals.shape[0])]
    pallas_call x1, Pallas kernels: 51.9 us -> 52.9 us  [body(): pl.pallas_call(functools.partial(multiply, rows, cols, part, depth, n_cop...]
where the time goes in v2:
time: 55.6 us; the launch traced here: 55.4 us
  Pallas kernels  52.9 us (95%)
  local copies, waits for them, and re-layouts  1.89 us (3%)
  between operations  0.66 us (1%)
    pallas_call x1, Pallas kernels, body(): pl.pallas_call(functools.partial(multiply, rows, cols, part, depth, n_cop...  52.9 us
    unnamed x1, local copies, waits for them, and re-layouts  1.89 us

profile of v2, /device:TPU:0, one launch (start us, length us, event | category | flops | bytes accessed | tf_op | source)
XLA Modules:
  0.0 55.4 jit_solution(16453286032950869246)
XLA Ops:
  0.7 52.9 %shard_map.64 = f32[128,1024]{1,0:T(8,128)} custom-call(s32[2,2,8]{2,1,0:T(2,128)} %bitcast.13, s32[2]{0:T(128)} %bitcast.15, s32[2,24]{1,0:T(2,128)} %bitcast.14, s32[1]{0:T(128)} %bitcast.10.refs_3_, f32[2,8,64,64]{3,2,1,0:T(8,128)} %bitcast.12, f32[24,64,64]{2,1,0:T(8,128)} %bitcast.11), custom_call_target="tpu_custom_call" | custom-call | tf_op jit(solution)/shard_map/pallas_call | solution.py:344
  53.5 1.9 %copy.9 = f32[128,1024]{1,0:T(8,128)} copy(f32[128,1024]{1,0:T(8,128)} %shard_map.64) | data formatting | bytes 1048576

commit v3 on v2

--- a/solution.py
+++ b/solution.py
@@ -28,13 +28,6 @@
     return high, (x - high.astype(jnp.float32)).astype(jnp.bfloat16)
 
 
-def dot(x, y):
-    xh, xl = halves(x)
-    yh, yl = halves(y)
-    f = functools.partial(jnp.dot, preferred_element_type=jnp.float32)
-    return f(xh, yh) + (f(xh, yl) + f(xl, yh))
-
-
 def powers(n):
     out, b = [], n // 2
     while b:
@@ -46,7 +39,7 @@
 def multiply(rows, cols, part, depth, n_copies, *refs):
     hbm, out_ref, held = refs[:6], refs[6], refs[7:13]
     a_pos, a_num, b_pos, b_num, a_val, b_val = held
-    a_full, b_full, sent, landed, send_sem, recv_sem, local_sem = refs[13:]
+    a_full, b_full, a_half, b_half, sent, landed, send_sem, recv_sem, local_sem = refs[13:]
     i, j, l = lax.axis_index("row"), lax.axis_index("col"), lax.axis_index("layer")
     row_bits, col_bits = powers(rows), powers(cols)
     slots = rows // cols
@@ -56,10 +49,9 @@
     is_outer = jnp.logical_or(l == 0, l == 3)
     inner_dest = 1 + l // 2
     outer_dest = 3 * (l // 2)
-    far_lo = pl.multiple_of(2 * part * (1 - l // 2), 2 * part)
+    dests = [3 - 3 * (l // 2), 2 - l // 2, outer_dest, inner_dest]
+    starts = [pl.multiple_of(part * dest, part) for dest in dests]
     near_lo = pl.multiple_of(2 * part * (l // 2), 2 * part)
-    inner_lo = pl.multiple_of(part * inner_dest, part)
-    outer_lo = pl.multiple_of(part * outer_dest, part)
 
     def flip(x, bit):
         return x + bit - 2 * bit * ((x // bit) % 2)
@@ -86,8 +78,8 @@
     def arrive(copies, cond=None):
         when(cond, lambda: [c.wait_recv() for c in copies] and None)
 
-    def depart(entry):
-        copies, cond = entry
+    def depart(copies, cond):
+        pending[:] = [p for p in pending if p[0] is not copies or p[1] is not cond]
         when(cond, lambda: [c.wait_send() for c in copies] and None)
 
     def at(piece):
@@ -184,6 +176,7 @@
         load.wait()
     a_dense()
     b_dense(0)
+    b_dense(1)
     pl.semaphore_wait(barrier, len(peers))
 
     def a_finish(q, lo, size, first, cond):
@@ -202,127 +195,166 @@
                 arrive(more, cond)
         return more
 
-    za_far, zb = z_a(far_lo, 2 * part), [z_b(c) for c in range(CHUNKS)]
-    za_inner = z_a(inner_lo, part)
-    start(za_far, is_outer)
-    far0 = a_stage(0, far_lo, 2 * part, 0)
-    start(far0, is_inner)
-    b0 = [None] * CHUNKS
-    b1 = [None] * CHUNKS
-    b0[0] = b_stage(0, 0, 0)
+    step = min(rows * depth, 512)
+
+    def steps(act):
+        total = rows * depth // step
+        if total == 1:
+            act(pl.ds(0, step))
+        else:
+            pl.loop(0, total)(lambda k: act(pl.ds(pl.multiple_of(k * step, step), step)))
+
+    def chunk(c):
+        return pl.ds(c * width, width)
+
+    def halve_a(q, n):
+        def act(k):
+            high, low = halves(a_full[q, pl.ds(starts[n], part), k])
+            a_half[q, n, pl.ds(0, part), k] = high
+            a_half[q, n, pl.ds(part, part), k] = low
+        steps(act)
+
+    def halve_b(q, c):
+        def act(k):
+            b_half[q, 0, k, chunk(c)], b_half[q, 1, k, chunk(c)] = halves(b_full[q, k, chunk(c)])
+        steps(act)
+
+    def product(layers, n, c, out):
+        def term(q, k):
+            first = jnp.dot(a_half[q, n, :, k], b_half[q, 0, k, chunk(c)], preferred_element_type=jnp.float32)
+            other = jnp.dot(a_half[q, n, pl.ds(0, part), k], b_half[q, 1, k, chunk(c)], preferred_element_type=jnp.float32)
+            return first[:part] + (first[part:] + other)
+
+        if rows * depth == step:
+            value = term(layers[0], pl.ds(0, step))
+            for q in layers[1:]:
+                value = value + term(q, pl.ds(0, step))
+            out[:, chunk(c)] = value
+        else:
+            out[:, chunk(c)] = jnp.zeros((part, width), jnp.float32)
+            for q in layers:
+                def act(k, q=q):
+                    out[:, chunk(c)] += term(q, k)
+                steps(act)
+
+    far_sent, near_sent = [], []
+    for c in range(CHUNKS):
+        far_sent.append([copy(sent.at[n, :, chunk(c)], landed.at[0, :, chunk(c)], {"layer": dests[n]}, n) for n in range(2)])
+        near_sent.append([copy(sent.at[2, :, chunk(c)], landed.at[1, :, chunk(c)], to_partner)])
+
+    def far_chunk(n, c):
+        when(is_inner, lambda: product((0, 1), n, c, sent.at[n]))
+        start([far_sent[c][n]], is_inner)
+
+    def near_chunk(c):
+        when(is_inner, lambda: product((0,), 2, c, sent.at[2]))
+        start(near_sent[c], is_inner)
+
+    def chunk_here(c):
+        arrive(last0[c])
+        arrive(last1[c], is_inner)
+        halve_b(0, c)
+        when(is_inner, lambda: halve_b(1, c))
+
+    def outer_chunk(c):
+        when(is_outer, lambda: product((0,), 2, c, out_ref))
+
+    za = [z_a(starts[n], part) for n in (0, 1, 3)]
+    zb = [z_b(c) for c in range(CHUNKS)]
+    fo0, fi0 = a_stage(0, starts[0], part, 0), a_stage(0, starts[1], part, 0)
+    fo1, fi1 = a_stage(1, starts[0], part, 0), a_stage(1, starts[1], part, 0)
+    near0, inner1 = a_stage(0, near_lo, 2 * part, 0), a_stage(1, starts[3], part, 0)
+    b0 = [b_stage(0, c, 0) for c in range(CHUNKS)]
+    b1 = [b_stage(1, c, 0) for c in range(CHUNKS)]
+    last0, last1 = [None] * CHUNKS, [None] * CHUNKS
+
+    start(za[0], is_outer)
+    start(fo0, is_inner)
     start(b0[0])
     start(zb[0], is_outer)
-    for c in range(1, CHUNKS):
+    start(near0, is_outer)
+    start(b0[1])
+    for c in range(2, CHUNKS):
         b_dense(c)
-    near0 = a_stage(0, near_lo, 2 * part, 0)
-    start(near0, is_outer)
-    last0 = [None] * CHUNKS
-    last1 = [None] * CHUNKS
     last0[0] = b_relay(0, 0, b0[0], None)
-    b0[1] = b_stage(0, 1, 0)
-    arrive(za_far, is_inner)
-    far1 = a_stage(1, far_lo, 2 * part, 0)
-    start(far1, is_inner)
+    arrive(za[0], is_inner)
+    start(fo1, is_inner)
+    start(fi0, is_inner)
+    depart(za[0], is_outer)
+    start(za[1], is_outer)
     arrive(zb[0], is_inner)
-    b1[0] = b_stage(1, 0, 0)
     start(b1[0], is_inner)
-    start(b0[1])
-    depart((za_far, is_outer))
-    pending.remove((za_far, is_outer))
+    depart(zb[0], is_outer)
     start(zb[1], is_outer)
+    last0[1] = b_relay(0, 1, b0[1], None)
+    start(b0[2])
+    a_finish(0, starts[0], part, fo0, is_inner)
+    a_finish(1, starts[0], part, fo1, is_inner)
+    when(is_inner, lambda: [halve_a(q, 0) for q in range(2)] and None)
     last1[0] = b_relay(1, 0, b1[0], is_inner)
-    a_finish(0, far_lo, 2 * part, far0, is_inner)
-    a_finish(1, far_lo, 2 * part, far1, is_inner)
+    arrive(za[1], is_inner)
+    start(fi1, is_inner)
     start(near0, is_inner)
-
-    step = min(rows * depth, 512)
-
-    def product(q, lo, size, c):
-        total = rows * depth // step
-
-        def term(k):
-            at_k = pl.ds(pl.multiple_of(k * step, step), step)
-            return dot(a_full[q, pl.ds(lo, size), at_k], b_full[q, at_k, pl.ds(c * width, width)])
-
-        if total == 1:
-            return term(0)
-        return lax.fori_loop(0, total, lambda k, s: s + term(k), jnp.zeros((size, width), jnp.float32))
-
-    def chunk(c):
-        return pl.ds(c * width, width)
-
-    results = []
-
-    def far_chunk(c):
-        def act():
-            value = product(0, far_lo, 2 * part, c) + product(1, far_lo, 2 * part, c)
-            sent[0, :, chunk(c)] = value[:part]
-            sent[1, :, chunk(c)] = value[part:]
-        when(is_inner, act)
-        first = 2 * (1 - l // 2)
-        copies = []
-        for n in range(2):
-            copies.append(copy(sent.at[n, :, chunk(c)], landed.at[0, :, chunk(c)], {"layer": first + n}, n))
-        start(copies, is_inner)
-        return copies[0]
-
-    def near_chunk(c):
-        def act():
-            sent[2, :, chunk(c)] = product(0, outer_lo, part, c)
-        when(is_inner, act)
-        copies = [copy(sent.at[2, :, chunk(c)], landed.at[1, :, chunk(c)], to_partner)]
-        start(copies, is_inner)
-        return copies[0]
-
-    def outer_chunk(c):
-        def act():
-            out_ref[:, chunk(c)] = product(0, outer_lo, part, c)
-        when(is_outer, act)
-
-    def inner_chunk(c):
-        def act():
-            out_ref[:, chunk(c)] = product(0, inner_lo, part, c) + product(1, inner_lo, part, c)
-        when(is_inner, act)
-
-    far_sent, near_sent = [None] * CHUNKS, [None] * CHUNKS
+    depart(za[1], is_outer)
+    start(zb[2], is_outer)
+    chunk_here(0)
+    far_chunk(0, 0)
+    arrive(zb[1], is_inner)
+    start(b1[1], is_inner)
+    depart(zb[1], is_outer)
+    start(zb[3], is_outer)
+    a_finish(0, starts[1], part, fi0, is_inner)
+    a_finish(1, starts[1], part, fi1, is_inner)
+    when(is_inner, lambda: [halve_a(q, 1) for q in range(2)] and None)
+    far_chunk(1, 0)
+    last0[2] = b_relay(0, 2, b0[2], None)
+    start(b0[3])
+    arrive(zb[2], is_inner)
+    start(b1[2], is_inner)
+    depart(zb[2], is_outer)
+    start(za[2], is_outer)
+    last1[1] = b_relay(1, 1, b1[1], is_inner)
+    chunk_here(1)
+    far_chunk(0, 1)
+    far_chunk(1, 1)
+    arrive(zb[3], is_inner)
+    start(b1[3], is_inner)
+    a_finish(0, near_lo, 2 * part, near0, None)
+    halve_a(0, 2)
+    when(is_inner, lambda: halve_a(0, 3))
+    near_chunk(0)
+    outer_chunk(0)
+    outer_chunk(1)
+    last0[3] = b_relay(0, 3, b0[3], None)
+    last1[2] = b_relay(1, 2, b1[2], is_inner)
+    chunk_here(2)
+    far_chunk(0, 2)
+    far_chunk(1, 2)
+    near_chunk(1)
+    outer_chunk(2)
+    arrive(za[2], is_inner)
+    start(inner1, is_inner)
+    last1[3] = b_relay(1, 3, b1[3], is_inner)
+    chunk_here(3)
+    far_chunk(0, 3)
+    far_chunk(1, 3)
+    near_chunk(2)
+    near_chunk(3)
+    outer_chunk(3)
+    a_finish(1, starts[3], part, inner1, is_inner)
+    when(is_inner, lambda: halve_a(1, 3))
     for c in range(CHUNKS):
-        if c + 1 < CHUNKS:
-            arrive(zb[c + 1], is_inner)
-            b1[c + 1] = b_stage(1, c + 1, 0)
-            start(b1[c + 1], is_inner)
-            if c + 2 < CHUNKS:
-                b0[c + 2] = b_stage(0, c + 2, 0)
-                start(b0[c + 2])
-                start(zb[c + 2], is_outer)
-            else:
-                start(za_inner, is_outer)
-        arrive(last0[c])
-        arrive(last1[c], is_inner)
-        far_sent[c] = far_chunk(c)
-        if c + 1 < CHUNKS:
-            last0[c + 1] = b_relay(0, c + 1, b0[c + 1], None)
-            last1[c + 1] = b_relay(1, c + 1, b1[c + 1], is_inner)
-        if c == 0:
-            a_finish(0, near_lo, 2 * part, near0, None)
-        else:
-            near_sent[c - 1] = near_chunk(c - 1)
-        outer_chunk(c)
-    near_sent[CHUNKS - 1] = near_chunk(CHUNKS - 1)
-    arrive(za_inner, is_inner)
-    inner1 = a_stage(1, inner_lo, part, 0)
-    start(inner1, is_inner)
-    a_finish(1, inner_lo, part, inner1, is_inner)
+        when(is_inner, lambda c=c: product((0, 1), 3, c, out_ref))
     for c in range(CHUNKS):
-        inner_chunk(c)
-        far_sent[c].wait_recv()
+        far_sent[c][0].wait_recv()
         out_ref[:, chunk(c)] += landed[0, :, chunk(c)]
 
         def add(c=c):
-            near_sent[c].wait_recv()
+            near_sent[c][0].wait_recv()
             out_ref[:, chunk(c)] += landed[1, :, chunk(c)]
         when(is_outer, add)
-    for entry in pending:
-        depart(entry)
+    for copies, cond in list(pending):
+        depart(copies, cond)
 
 
 def body(rows, cols, a_values, a_places, a_counts, b_values, b_places, b_counts):
@@ -340,7 +372,7 @@
     full_rows, full_cols = TILE_ROWS * width, tile_cols * width
     f32 = jnp.float32
     vmem = pl.BlockSpec(memory_space=pltpu.VMEM)
-    n_copies = 2 * CHUNKS * (rows - 1) + 4 * slots * (cols - 1) + 2 * slots + CHUNKS * 4
+    n_copies = 2 * CHUNKS * (rows - 1) + 6 * slots * (cols - 1) + 3 * slots + 4 * CHUNKS
     return pl.pallas_call(
         functools.partial(multiply, rows, cols, part, depth, n_copies),
         out_shape=jax.ShapeDtypeStruct((part, full_cols), f32),
@@ -352,6 +384,8 @@
             pltpu.VMEM(b_vals.shape, f32),
             pltpu.VMEM((2, full_rows, rows * depth), f32),
             pltpu.VMEM((2, rows * depth, full_cols), f32),
+            pltpu.VMEM((2, layers, 2 * part, rows * depth), jnp.bfloat16),
+            pltpu.VMEM((2, 2, rows * depth, full_cols), jnp.bfloat16),
             pltpu.VMEM((3, part, full_cols), f32),
             pltpu.VMEM((2, part, full_cols), f32),
             pltpu.SemaphoreType.DMA((n_copies,)),

time: 55.6 us -> 52.7 us (0.948)
  Pallas kernels: 52.9 us -> 49.9 us
    pallas_call x1, Pallas kernels: 52.9 us -> 49.9 us  [body(): pl.pallas_call(functools.partial(multiply, rows, cols, part, depth, n_cop...]
where the time goes in v3:
time: 52.7 us; the launch traced here: 52.5 us
  Pallas kernels  49.9 us (95%)
  local copies, waits for them, and re-layouts  1.89 us (4%)
  between operations  0.66 us (1%)
    pallas_call x1, Pallas kernels, body(): pl.pallas_call(functools.partial(multiply, rows, cols, part, depth, n_cop...  49.9 us
    unnamed x1, local copies, waits for them, and re-layouts  1.89 us

profile of v3, /device:TPU:0, one launch (start us, length us, event | category | flops | bytes accessed | tf_op | source)
XLA Modules:
  0.0 52.5 jit_solution(1598919658785737982)
XLA Ops:
  0.7 49.9 %shard_map.64 = f32[128,1024]{1,0:T(8,128)} custom-call(s32[2,2,8]{2,1,0:T(2,128)} %bitcast.13, s32[2]{0:T(128)} %bitcast.15, s32[2,24]{1,0:T(2,128)} %bitcast.14, s32[1]{0:T(128)} %bitcast.10.refs_3_, f32[2,8,64,64]{3,2,1,0:T(8,128)} %bitcast.12, f32[24,64,64]{2,1,0:T(8,128)} %bitcast.11), custom_call_target="tpu_custom_call" | custom-call | tf_op jit(solution)/shard_map/pallas_call | solution.py:376
  50.6 1.9 %copy.9 = f32[128,1024]{1,0:T(8,128)} copy(f32[128,1024]{1,0:T(8,128)} %shard_map.64) | data formatting | bytes 1048576

commit v4 on v3

--- a/solution.py
+++ b/solution.py
@@ -43,7 +43,7 @@
     i, j, l = lax.axis_index("row"), lax.axis_index("col"), lax.axis_index("layer")
     row_bits, col_bits = powers(rows), powers(cols)
     slots = rows // cols
-    width = b_full.shape[2] // CHUNKS
+    width = b_full.shape[3]
     partner = l + 1 - 2 * (l % 2)
     is_inner = jnp.logical_or(l == 1, l == 2)
     is_outer = jnp.logical_or(l == 0, l == 3)
@@ -86,7 +86,7 @@
         return pl.ds(pl.multiple_of(piece * depth, depth), depth)
 
     def b_view(q, piece, c):
-        return b_full.at[q, at(piece), pl.ds(c * width, width)]
+        return b_full.at[q, c, at(piece)]
 
     def b_stage(q, c, stage):
         bit = row_bits[stage]
@@ -105,7 +105,7 @@
         return copies
 
     def a_view(q, lo, size, piece):
-        return a_full.at[q, pl.ds(lo, size), at(piece)]
+        return a_full.at[q, piece, pl.ds(lo, size)]
 
     def a_stage(q, lo, size, stage):
         bit = col_bits[stage]
@@ -144,7 +144,7 @@
         load.wait()
 
     block = a_val.shape[-1]
-    inner, tile_cols = depth // block, b_full.shape[2] // block
+    inner, tile_cols = depth // block, CHUNKS * width // block
     caps = a_val.shape[1]
     a_slot = [
         inverse([jnp.where(s < a_num[m], a_pos[m, 0, s] * inner + a_pos[m, 1, s], -1) for s in range(caps)],
@@ -163,14 +163,14 @@
         for m in range(slots):
             for r in range(TILE_ROWS):
                 parts = [stored(a_val.at[m], a_slot[m][r * inner + k]) for k in range(inner)]
-                a_full[0, pl.ds(r * block, block), at(my_pieces[m])] = jnp.concatenate(parts, 1)
+                a_full[0, my_pieces[m], pl.ds(r * block, block)] = jnp.concatenate(parts, 1)
 
     def b_dense(c):
         for r in range(inner):
             rows_r = pl.ds(pl.multiple_of(my_pieces[0] * depth + r * block, block), block)
             for k in range(c * width // block, (c + 1) * width // block, 2):
                 parts = [stored(b_val, b_slot[r * tile_cols + k + d]) for d in range(2)]
-                b_full[0, rows_r, pl.ds(k * block, 2 * block)] = jnp.concatenate(parts, 1)
+                b_full[0, c, rows_r, pl.ds(k * block - c * width, 2 * block)] = jnp.concatenate(parts, 1)
 
     for load in loads[4:]:
         load.wait()
@@ -208,46 +208,51 @@
         return pl.ds(c * width, width)
 
     def halve_a(q, n):
-        def act(k):
-            high, low = halves(a_full[q, pl.ds(starts[n], part), k])
+        def act(piece):
+            k = at(piece)
+            high, low = halves(a_full[q, piece, pl.ds(starts[n], part)])
             a_half[q, n, pl.ds(0, part), k] = high
             a_half[q, n, pl.ds(part, part), k] = low
-        steps(act)
+        if rows <= 4:
+            for piece in range(rows):
+                act(piece)
+        else:
+            pl.loop(0, rows)(act)
 
     def halve_b(q, c):
         def act(k):
-            b_half[q, 0, k, chunk(c)], b_half[q, 1, k, chunk(c)] = halves(b_full[q, k, chunk(c)])
+            b_half[q, 0, c, k], b_half[q, 1, c, k] = halves(b_full[q, c, k])
         steps(act)
 
     def product(layers, n, c, out):
         def term(q, k):
-            first = jnp.dot(a_half[q, n, :, k], b_half[q, 0, k, chunk(c)], preferred_element_type=jnp.float32)
-            other = jnp.dot(a_half[q, n, pl.ds(0, part), k], b_half[q, 1, k, chunk(c)], preferred_element_type=jnp.float32)
+            first = jnp.dot(a_half[q, n, :, k], b_half[q, 0, c, k], preferred_element_type=jnp.float32)
+            other = jnp.dot(a_half[q, n, pl.ds(0, part), k], b_half[q, 1, c, k], preferred_element_type=jnp.float32)
             return first[:part] + (first[part:] + other)
 
         if rows * depth == step:
             value = term(layers[0], pl.ds(0, step))
             for q in layers[1:]:
                 value = value + term(q, pl.ds(0, step))
-            out[:, chunk(c)] = value
+            out[...] = value
         else:
-            out[:, chunk(c)] = jnp.zeros((part, width), jnp.float32)
+            out[...] = jnp.zeros((part, width), jnp.float32)
             for q in layers:
                 def act(k, q=q):
-                    out[:, chunk(c)] += term(q, k)
+                    out[...] += term(q, k)
                 steps(act)
 
     far_sent, near_sent = [], []
     for c in range(CHUNKS):
-        far_sent.append([copy(sent.at[n, :, chunk(c)], landed.at[0, :, chunk(c)], {"layer": dests[n]}, n) for n in range(2)])
-        near_sent.append([copy(sent.at[2, :, chunk(c)], landed.at[1, :, chunk(c)], to_partner)])
+        far_sent.append([copy(sent.at[n, c], landed.at[0, c], {"layer": dests[n]}, n) for n in range(2)])
+        near_sent.append([copy(sent.at[2, c], landed.at[1, c], to_partner)])
 
     def far_chunk(n, c):
-        when(is_inner, lambda: product((0, 1), n, c, sent.at[n]))
+        when(is_inner, lambda: product((0, 1), n, c, sent.at[n, c]))
         start([far_sent[c][n]], is_inner)
 
     def near_chunk(c):
-        when(is_inner, lambda: product((0,), 2, c, sent.at[2]))
+        when(is_inner, lambda: product((0,), 2, c, sent.at[2, c]))
         start(near_sent[c], is_inner)
 
     def chunk_here(c):
@@ -257,7 +262,7 @@
         when(is_inner, lambda: halve_b(1, c))
 
     def outer_chunk(c):
-        when(is_outer, lambda: product((0,), 2, c, out_ref))
+        when(is_outer, lambda: product((0,), 2, c, out_ref.at[:, chunk(c)]))
 
     za = [z_a(starts[n], part) for n in (0, 1, 3)]
     zb = [z_b(c) for c in range(CHUNKS)]
@@ -344,14 +349,14 @@
     a_finish(1, starts[3], part, inner1, is_inner)
     when(is_inner, lambda: halve_a(1, 3))
     for c in range(CHUNKS):
-        when(is_inner, lambda c=c: product((0, 1), 3, c, out_ref))
+        when(is_inner, lambda c=c: product((0, 1), 3, c, out_ref.at[:, chunk(c)]))
     for c in range(CHUNKS):
         far_sent[c][0].wait_recv()
-        out_ref[:, chunk(c)] += landed[0, :, chunk(c)]
+        out_ref[:, chunk(c)] += landed[0, c]
 
         def add(c=c):
             near_sent[c][0].wait_recv()
-            out_ref[:, chunk(c)] += landed[1, :, chunk(c)]
+            out_ref[:, chunk(c)] += landed[1, c]
         when(is_outer, add)
     for copies, cond in list(pending):
         depart(copies, cond)
@@ -360,7 +365,7 @@
 def body(rows, cols, a_values, a_places, a_counts, b_values, b_places, b_counts):
     a_vals = a_values.reshape(a_values.shape[3:])
     b_vals = b_values.reshape(b_values.shape[3:])
-    slots, width = a_vals.shape[0], a_vals.shape[2]
+    slots, block = a_vals.shape[0], a_vals.shape[2]
     layers = lax.axis_size("layer")
     inner = TILE_ROWS // layers
     tile_cols = TILE_ROWS * rows // cols
@@ -368,8 +373,9 @@
     a_num = a_counts.reshape(slots)
     b_pos = b_places.reshape(b_places.shape[3:]).T
     b_num = b_counts.reshape(1)
-    depth, part = inner * width, TILE_ROWS * width // layers
-    full_rows, full_cols = TILE_ROWS * width, tile_cols * width
+    depth, part = inner * block, TILE_ROWS * block // layers
+    full_rows, full_cols = TILE_ROWS * block, tile_cols * block
+    width = full_cols // CHUNKS
     f32 = jnp.float32
     vmem = pl.BlockSpec(memory_space=pltpu.VMEM)
     n_copies = 2 * CHUNKS * (rows - 1) + 6 * slots * (cols - 1) + 3 * slots + 4 * CHUNKS
@@ -382,12 +388,12 @@
             *[pltpu.SMEM(x.shape, jnp.int32) for x in (a_pos, a_num, b_pos, b_num)],
             pltpu.VMEM(a_vals.shape, f32),
             pltpu.VMEM(b_vals.shape, f32),
-            pltpu.VMEM((2, full_rows, rows * depth), f32),
-            pltpu.VMEM((2, rows * depth, full_cols), f32),
+            pltpu.VMEM((2, rows, full_rows, depth), f32),
+            pltpu.VMEM((2, CHUNKS, rows * depth, width), f32),
             pltpu.VMEM((2, layers, 2 * part, rows * depth), jnp.bfloat16),
-            pltpu.VMEM((2, 2, rows * depth, full_cols), jnp.bfloat16),
-            pltpu.VMEM((3, part, full_cols), f32),
-            pltpu.VMEM((2, part, full_cols), f32),
+            pltpu.VMEM((2, 2, CHUNKS, rows * depth, width), jnp.bfloat16),
+            pltpu.VMEM((3, CHUNKS, part, width), f32),
+            pltpu.VMEM((2, CHUNKS, part, width), f32),
             pltpu.SemaphoreType.DMA((n_copies,)),
             pltpu.SemaphoreType.DMA((n_copies,)),
             pltpu.SemaphoreType.DMA((6,)),

time: 52.7 us -> 52.5 us (level)
  no operation moved by 1% of the time
where the time goes in v4:
time: 52.5 us; the launch traced here: 52.3 us
  Pallas kernels  49.8 us (95%)
  local copies, waits for them, and re-layouts  1.89 us (4%)
  between operations  0.66 us (1%)
    pallas_call x1, Pallas kernels, body(): pl.pallas_call(functools.partial(multiply, rows, cols, part, depth, n_cop...  49.8 us
    unnamed x1, local copies, waits for them, and re-layouts  1.89 us

profile of v4, /device:TPU:0, one launch (start us, length us, event | category | flops | bytes accessed | tf_op | source)
XLA Modules:
  0.0 52.3 jit_solution(3432368248252453227)
XLA Ops:
  0.7 49.8 %shard_map.64 = f32[128,1024]{1,0:T(8,128)} custom-call(s32[2,2,8]{2,1,0:T(2,128)} %bitcast.13, s32[2]{0:T(128)} %bitcast.15, s32[2,24]{1,0:T(2,128)} %bitcast.14, s32[1]{0:T(128)} %bitcast.10.refs_3_, f32[2,8,64,64]{3,2,1,0:T(8,128)} %bitcast.12, f32[24,64,64]{2,1,0:T(8,128)} %bitcast.11), custom_call_target="tpu_custom_call" | custom-call | tf_op jit(solution)/shard_map/pallas_call | solution.py:382
  50.4 1.9 %copy.9 = f32[128,1024]{1,0:T(8,128)} copy(f32[128,1024]{1,0:T(8,128)} %shard_map.64) | data formatting | bytes 1048576

commit v5 on v4

--- a/solution.py
+++ b/solution.py
@@ -9,7 +9,11 @@
 
 MESH = pl.DeviceIdType.MESH
 TILE_ROWS = 8
-CHUNKS = 4
+
+
+def chunk_widths(total):
+    unit = total // 8
+    return [unit] + [2 * unit] * 3 + [unit]
 
 
 def inverse(spots, total, bits):
@@ -43,7 +47,8 @@
     i, j, l = lax.axis_index("row"), lax.axis_index("col"), lax.axis_index("layer")
     row_bits, col_bits = powers(rows), powers(cols)
     slots = rows // cols
-    width = b_full.shape[3]
+    widths = chunk_widths(b_full.shape[2])
+    n_chunks = len(widths)
     partner = l + 1 - 2 * (l % 2)
     is_inner = jnp.logical_or(l == 1, l == 2)
     is_outer = jnp.logical_or(l == 0, l == 3)
@@ -86,7 +91,10 @@
         return pl.ds(pl.multiple_of(piece * depth, depth), depth)
 
     def b_view(q, piece, c):
-        return b_full.at[q, c, at(piece)]
+        return b_full.at[q, at(piece), chunk(c)]
+
+    def chunk(c):
+        return pl.ds(sum(widths[:c]), widths[c])
 
     def b_stage(q, c, stage):
         bit = row_bits[stage]
@@ -144,7 +152,7 @@
         load.wait()
 
     block = a_val.shape[-1]
-    inner, tile_cols = depth // block, CHUNKS * width // block
+    inner, tile_cols = depth // block, b_full.shape[2] // block
     caps = a_val.shape[1]
     a_slot = [
         inverse([jnp.where(s < a_num[m], a_pos[m, 0, s] * inner + a_pos[m, 1, s], -1) for s in range(caps)],
@@ -168,9 +176,9 @@
     def b_dense(c):
         for r in range(inner):
             rows_r = pl.ds(pl.multiple_of(my_pieces[0] * depth + r * block, block), block)
-            for k in range(c * width // block, (c + 1) * width // block, 2):
+            for k in range(sum(widths[:c]) // block, sum(widths[:c + 1]) // block, 2):
                 parts = [stored(b_val, b_slot[r * tile_cols + k + d]) for d in range(2)]
-                b_full[0, c, rows_r, pl.ds(k * block - c * width, 2 * block)] = jnp.concatenate(parts, 1)
+                b_full[0, rows_r, pl.ds(k * block, 2 * block)] = jnp.concatenate(parts, 1)
 
     for load in loads[4:]:
         load.wait()
@@ -203,9 +211,6 @@
             act(pl.ds(0, step))
         else:
             pl.loop(0, total)(lambda k: act(pl.ds(pl.multiple_of(k * step, step), step)))
-
-    def chunk(c):
-        return pl.ds(c * width, width)
 
     def halve_a(q, n):
         def act(piece):
@@ -221,13 +226,13 @@
 
     def halve_b(q, c):
         def act(k):
-            b_half[q, 0, c, k], b_half[q, 1, c, k] = halves(b_full[q, c, k])
+            b_half[q, 0, k, chunk(c)], b_half[q, 1, k, chunk(c)] = halves(b_full[q, k, chunk(c)])
         steps(act)
 
     def product(layers, n, c, out):
         def term(q, k):
-            first = jnp.dot(a_half[q, n, :, k], b_half[q, 0, c, k], preferred_element_type=jnp.float32)
-            other = jnp.dot(a_half[q, n, pl.ds(0, part), k], b_half[q, 1, c, k], preferred_element_type=jnp.float32)
+            first = jnp.dot(a_half[q, n, :, k], b_half[q, 0, k, chunk(c)], preferred_element_type=jnp.float32)
+            other = jnp.dot(a_half[q, n, pl.ds(0, part), k], b_half[q, 1, k, chunk(c)], preferred_element_type=jnp.float32)
             return first[:part] + (first[part:] + other)
 
         if rows * depth == step:
@@ -236,23 +241,23 @@
                 value = value + term(q, pl.ds(0, step))
             out[...] = value
         else:
-            out[...] = jnp.zeros((part, width), jnp.float32)
+            out[...] = jnp.zeros((part, widths[c]), jnp.float32)
             for q in layers:
                 def act(k, q=q):
                     out[...] += term(q, k)
                 steps(act)
 
     far_sent, near_sent = [], []
-    for c in range(CHUNKS):
-        far_sent.append([copy(sent.at[n, c], landed.at[0, c], {"layer": dests[n]}, n) for n in range(2)])
-        near_sent.append([copy(sent.at[2, c], landed.at[1, c], to_partner)])
+    for c in range(n_chunks):
+        far_sent.append([copy(sent.at[n, :, chunk(c)], landed.at[0, :, chunk(c)], {"layer": dests[n]}, n) for n in range(2)])
+        near_sent.append([copy(sent.at[2, :, chunk(c)], landed.at[1, :, chunk(c)], to_partner)])
 
     def far_chunk(n, c):
-        when(is_inner, lambda: product((0, 1), n, c, sent.at[n, c]))
+        when(is_inner, lambda: product((0, 1), n, c, sent.at[n, :, chunk(c)]))
         start([far_sent[c][n]], is_inner)
 
     def near_chunk(c):
-        when(is_inner, lambda: product((0,), 2, c, sent.at[2, c]))
+        when(is_inner, lambda: product((0,), 2, c, sent.at[2, :, chunk(c)]))
         start(near_sent[c], is_inner)
 
     def chunk_here(c):
@@ -265,32 +270,40 @@
         when(is_outer, lambda: product((0,), 2, c, out_ref.at[:, chunk(c)]))
 
     za = [z_a(starts[n], part) for n in (0, 1, 3)]
-    zb = [z_b(c) for c in range(CHUNKS)]
+    zb = [z_b(c) for c in range(n_chunks)]
     fo0, fi0 = a_stage(0, starts[0], part, 0), a_stage(0, starts[1], part, 0)
     fo1, fi1 = a_stage(1, starts[0], part, 0), a_stage(1, starts[1], part, 0)
     near0, inner1 = a_stage(0, near_lo, 2 * part, 0), a_stage(1, starts[3], part, 0)
-    b0 = [b_stage(0, c, 0) for c in range(CHUNKS)]
-    b1 = [b_stage(1, c, 0) for c in range(CHUNKS)]
-    last0, last1 = [None] * CHUNKS, [None] * CHUNKS
-
-    start(za[0], is_outer)
+    b0 = [b_stage(0, c, 0) for c in range(n_chunks)]
+    b1 = [b_stage(1, c, 0) for c in range(n_chunks)]
+    last0, last1 = [None] * n_chunks, [None] * n_chunks
+
+    z_queue = [za[0], zb[0], za[1]] + zb[1:] + [za[2]]
+    z_started = []
+
+    def more_z():
+        if len(z_started) >= 2:
+            depart(z_started[-2], is_outer)
+        if len(z_started) < len(z_queue):
+            start(z_queue[len(z_started)], is_outer)
+            z_started.append(z_queue[len(z_started)])
+
+    more_z()
     start(fo0, is_inner)
     start(b0[0])
-    start(zb[0], is_outer)
+    more_z()
     start(near0, is_outer)
     start(b0[1])
-    for c in range(2, CHUNKS):
+    for c in range(2, n_chunks):
         b_dense(c)
     last0[0] = b_relay(0, 0, b0[0], None)
     arrive(za[0], is_inner)
     start(fo1, is_inner)
     start(fi0, is_inner)
-    depart(za[0], is_outer)
-    start(za[1], is_outer)
+    more_z()
     arrive(zb[0], is_inner)
     start(b1[0], is_inner)
-    depart(zb[0], is_outer)
-    start(zb[1], is_outer)
+    more_z()
     last0[1] = b_relay(0, 1, b0[1], None)
     start(b0[2])
     a_finish(0, starts[0], part, fo0, is_inner)
@@ -300,63 +313,52 @@
     arrive(za[1], is_inner)
     start(fi1, is_inner)
     start(near0, is_inner)
-    depart(za[1], is_outer)
-    start(zb[2], is_outer)
+    more_z()
     chunk_here(0)
     far_chunk(0, 0)
     arrive(zb[1], is_inner)
     start(b1[1], is_inner)
-    depart(zb[1], is_outer)
-    start(zb[3], is_outer)
+    more_z()
     a_finish(0, starts[1], part, fi0, is_inner)
     a_finish(1, starts[1], part, fi1, is_inner)
     when(is_inner, lambda: [halve_a(q, 1) for q in range(2)] and None)
     far_chunk(1, 0)
-    last0[2] = b_relay(0, 2, b0[2], None)
-    start(b0[3])
-    arrive(zb[2], is_inner)
-    start(b1[2], is_inner)
-    depart(zb[2], is_outer)
-    start(za[2], is_outer)
-    last1[1] = b_relay(1, 1, b1[1], is_inner)
-    chunk_here(1)
-    far_chunk(0, 1)
-    far_chunk(1, 1)
-    arrive(zb[3], is_inner)
-    start(b1[3], is_inner)
-    a_finish(0, near_lo, 2 * part, near0, None)
-    halve_a(0, 2)
-    when(is_inner, lambda: halve_a(0, 3))
-    near_chunk(0)
-    outer_chunk(0)
-    outer_chunk(1)
-    last0[3] = b_relay(0, 3, b0[3], None)
-    last1[2] = b_relay(1, 2, b1[2], is_inner)
-    chunk_here(2)
-    far_chunk(0, 2)
-    far_chunk(1, 2)
-    near_chunk(1)
-    outer_chunk(2)
-    arrive(za[2], is_inner)
-    start(inner1, is_inner)
-    last1[3] = b_relay(1, 3, b1[3], is_inner)
-    chunk_here(3)
-    far_chunk(0, 3)
-    far_chunk(1, 3)
-    near_chunk(2)
-    near_chunk(3)
-    outer_chunk(3)
+    for c in range(1, n_chunks):
+        if c + 1 < n_chunks:
+            last0[c + 1] = b_relay(0, c + 1, b0[c + 1], None)
+            if c + 2 < n_chunks:
+                start(b0[c + 2])
+            arrive(zb[c + 1], is_inner)
+            start(b1[c + 1], is_inner)
+            more_z()
+        else:
+            arrive(za[2], is_inner)
+            start(inner1, is_inner)
+        last1[c] = b_relay(1, c, b1[c], is_inner)
+        chunk_here(c)
+        far_chunk(0, c)
+        far_chunk(1, c)
+        if c == 2:
+            a_finish(0, near_lo, 2 * part, near0, None)
+            halve_a(0, 2)
+            when(is_inner, lambda: halve_a(0, 3))
+        if c >= 2:
+            near_chunk(c - 2)
+            outer_chunk(c - 2)
+    for c in range(n_chunks - 2, n_chunks):
+        near_chunk(c)
+        outer_chunk(c)
     a_finish(1, starts[3], part, inner1, is_inner)
     when(is_inner, lambda: halve_a(1, 3))
-    for c in range(CHUNKS):
+    for c in range(n_chunks):
         when(is_inner, lambda c=c: product((0, 1), 3, c, out_ref.at[:, chunk(c)]))
-    for c in range(CHUNKS):
+    for c in range(n_chunks):
         far_sent[c][0].wait_recv()
-        out_ref[:, chunk(c)] += landed[0, c]
+        out_ref[:, chunk(c)] += landed[0, :, chunk(c)]
 
         def add(c=c):
             near_sent[c][0].wait_recv()
-            out_ref[:, chunk(c)] += landed[1, c]
+            out_ref[:, chunk(c)] += landed[1, :, chunk(c)]
         when(is_outer, add)
     for copies, cond in list(pending):
         depart(copies, cond)
@@ -375,10 +377,10 @@
     b_num = b_counts.reshape(1)
     depth, part = inner * block, TILE_ROWS * block // layers
     full_rows, full_cols = TILE_ROWS * block, tile_cols * block
-    width = full_cols // CHUNKS
+    chunks = len(chunk_widths(full_cols))
     f32 = jnp.float32
     vmem = pl.BlockSpec(memory_space=pltpu.VMEM)
-    n_copies = 2 * CHUNKS * (rows - 1) + 6 * slots * (cols - 1) + 3 * slots + 4 * CHUNKS
+    n_copies = 2 * chunks * (rows - 1) + 6 * slots * (cols - 1) + 3 * slots + 4 * chunks
     return pl.pallas_call(
         functools.partial(multiply, rows, cols, part, depth, n_copies),
         out_shape=jax.ShapeDtypeStruct((part, full_cols), f32),
@@ -389,11 +391,11 @@
             pltpu.VMEM(a_vals.shape, f32),
             pltpu.VMEM(b_vals.shape, f32),
             pltpu.VMEM((2, rows, full_rows, depth), f32),
-            pltpu.VMEM((2, CHUNKS, rows * depth, width), f32),
+            pltpu.VMEM((2, rows * depth, full_cols), f32),
             pltpu.VMEM((2, layers, 2 * part, rows * depth), jnp.bfloat16),
-            pltpu.VMEM((2, 2, CHUNKS, rows * depth, width), jnp.bfloat16),
-            pltpu.VMEM((3, CHUNKS, part, width), f32),
-            pltpu.VMEM((2, CHUNKS, part, width), f32),
+            pltpu.VMEM((2, 2, rows * depth, full_cols), jnp.bfloat16),
+            pltpu.VMEM((3, part, full_cols), f32),
+            pltpu.VMEM((2, part, full_cols), f32),
             pltpu.SemaphoreType.DMA((n_copies,)),
             pltpu.SemaphoreType.DMA((n_copies,)),
             pltpu.SemaphoreType.DMA((6,)),

time: 52.5 us -> 54.4 us (1.036)
  Pallas kernels: 49.8 us -> 51.5 us
    pallas_call x1, Pallas kernels: 49.8 us -> 51.5 us  [body(): pl.pallas_call(functools.partial(multiply, rows, cols, part, depth, n_cop...]
where the time goes in v5:
time: 54.4 us; the launch traced here: 54 us
  Pallas kernels  51.5 us (95%)
  local copies, waits for them, and re-layouts  1.89 us (3%)
  between operations  0.66 us (1%)
    pallas_call x1, Pallas kernels, body(): pl.pallas_call(functools.partial(multiply, rows, cols, part, depth, n_cop...  51.5 us
    unnamed x1, local copies, waits for them, and re-layouts  1.89 us

profile of v5, /device:TPU:0, one launch (start us, length us, event | category | flops | bytes accessed | tf_op | source)
XLA Modules:
  0.0 54.0 jit_solution(2555546893192305819)
XLA Ops:
  0.7 51.5 %shard_map.64 = f32[128,1024]{1,0:T(8,128)} custom-call(s32[2,2,8]{2,1,0:T(2,128)} %bitcast.13, s32[2]{0:T(128)} %bitcast.15, s32[2,24]{1,0:T(2,128)} %bitcast.14, s32[1]{0:T(128)} %bitcast.10.refs_3_, f32[2,8,64,64]{3,2,1,0:T(8,128)} %bitcast.12, f32[24,64,64]{2,1,0:T(8,128)} %bitcast.11), custom_call_target="tpu_custom_call" | custom-call | tf_op jit(solution)/shard_map/pallas_call | solution.py:384
  52.1 1.9 %copy.9 = f32[128,1024]{1,0:T(8,128)} copy(f32[128,1024]{1,0:T(8,128)} %shard_map.64) | data formatting | bytes 1048576

commit v6 on v5

--- a/solution.py
+++ b/solution.py
@@ -12,8 +12,8 @@
 
 
 def chunk_widths(total):
-    unit = total // 8
-    return [unit] + [2 * unit] * 3 + [unit]
+    unit = total // 4
+    return [unit, 2 * unit, unit]
 
 
 def inverse(spots, total, bits):

time: 54.4 us -> 57.2 us (1.051)
  Pallas kernels: 51.5 us -> 54.5 us
    pallas_call x1, Pallas kernels: 51.5 us -> 54.5 us  [body(): pl.pallas_call(functools.partial(multiply, rows, cols, part, depth, n_cop...]
where the time goes in v6:
time: 57.2 us; the launch traced here: 57 us
  Pallas kernels  54.5 us (95%)
  local copies, waits for them, and re-layouts  1.89 us (3%)
  between operations  0.66 us (1%)
    pallas_call x1, Pallas kernels, body(): pl.pallas_call(functools.partial(multiply, rows, cols, part, depth, n_cop...  54.5 us
    unnamed x1, local copies, waits for them, and re-layouts  1.89 us

profile of v6, /device:TPU:0, one launch (start us, length us, event | category | flops | bytes accessed | tf_op | source)
XLA Modules:
  0.0 57.0 jit_solution(16886768621488965879)
XLA Ops:
  0.7 54.5 %shard_map.64 = f32[128,1024]{1,0:T(8,128)} custom-call(s32[2,2,8]{2,1,0:T(2,128)} %bitcast.13, s32[2]{0:T(128)} %bitcast.15, s32[2,24]{1,0:T(2,128)} %bitcast.14, s32[1]{0:T(128)} %bitcast.10.refs_3_, f32[2,8,64,64]{3,2,1,0:T(8,128)} %bitcast.12, f32[24,64,64]{2,1,0:T(8,128)} %bitcast.11), custom_call_target="tpu_custom_call" | custom-call | tf_op jit(solution)/shard_map/pallas_call | solution.py:384
  55.1 1.9 %copy.9 = f32[128,1024]{1,0:T(8,128)} copy(f32[128,1024]{1,0:T(8,128)} %shard_map.64) | data formatting | bytes 1048576

commit v7 on v4

--- a/solution.py
+++ b/solution.py
@@ -277,6 +277,7 @@
     start(fo0, is_inner)
     start(b0[0])
     start(zb[0], is_outer)
+    start(za[1], is_outer)
     start(near0, is_outer)
     start(b0[1])
     for c in range(2, CHUNKS):
@@ -285,14 +286,15 @@
     arrive(za[0], is_inner)
     start(fo1, is_inner)
     start(fi0, is_inner)
+    start(b0[2])
     depart(za[0], is_outer)
-    start(za[1], is_outer)
+    start(zb[1], is_outer)
     arrive(zb[0], is_inner)
     start(b1[0], is_inner)
     depart(zb[0], is_outer)
-    start(zb[1], is_outer)
+    start(zb[2], is_outer)
     last0[1] = b_relay(0, 1, b0[1], None)
-    start(b0[2])
+    start(b0[3])
     a_finish(0, starts[0], part, fo0, is_inner)
     a_finish(1, starts[0], part, fo1, is_inner)
     when(is_inner, lambda: [halve_a(q, 0) for q in range(2)] and None)
@@ -301,23 +303,20 @@
     start(fi1, is_inner)
     start(near0, is_inner)
     depart(za[1], is_outer)
-    start(zb[2], is_outer)
+    start(zb[3], is_outer)
     chunk_here(0)
     far_chunk(0, 0)
     arrive(zb[1], is_inner)
     start(b1[1], is_inner)
     depart(zb[1], is_outer)
-    start(zb[3], is_outer)
+    start(za[2], is_outer)
     a_finish(0, starts[1], part, fi0, is_inner)
     a_finish(1, starts[1], part, fi1, is_inner)
     when(is_inner, lambda: [halve_a(q, 1) for q in range(2)] and None)
     far_chunk(1, 0)
     last0[2] = b_relay(0, 2, b0[2], None)
-    start(b0[3])
     arrive(zb[2], is_inner)
     start(b1[2], is_inner)
-    depart(zb[2], is_outer)
-    start(za[2], is_outer)
     last1[1] = b_relay(1, 1, b1[1], is_inner)
     chunk_here(1)
     far_chunk(0, 1)

time: 52.5 us -> 53.7 us (1.023)
  Pallas kernels: 49.8 us -> 51 us
    pallas_call x1, Pallas kernels: 49.8 us -> 51 us  [body(): pl.pallas_call(functools.partial(multiply, rows, cols, part, depth, n_cop...]
where the time goes in v7:
time: 53.7 us; the launch traced here: 53.5 us
  Pallas kernels  51 us (95%)
  local copies, waits for them, and re-layouts  1.89 us (4%)
  between operations  0.66 us (1%)
    pallas_call x1, Pallas kernels, body(): pl.pallas_call(functools.partial(multiply, rows, cols, part, depth, n_cop...  51 us
    unnamed x1, local copies, waits for them, and re-layouts  1.89 us

profile of v7, /device:TPU:0, one launch (start us, length us, event | category | flops | bytes accessed | tf_op | source)
XLA Modules:
  0.0 53.5 jit_solution(483309591290110092)
XLA Ops:
  0.7 51.0 %shard_map.64 = f32[128,1024]{1,0:T(8,128)} custom-call(s32[2,2,8]{2,1,0:T(2,128)} %bitcast.13, s32[2]{0:T(128)} %bitcast.15, s32[2,24]{1,0:T(2,128)} %bitcast.14, s32[1]{0:T(128)} %bitcast.10.refs_3_, f32[2,8,64,64]{3,2,1,0:T(8,128)} %bitcast.12, f32[24,64,64]{2,1,0:T(8,128)} %bitcast.11), custom_call_target="tpu_custom_call" | custom-call | tf_op jit(solution)/shard_map/pallas_call | solution.py:381
  51.7 1.9 %copy.9 = f32[128,1024]{1,0:T(8,128)} copy(f32[128,1024]{1,0:T(8,128)} %shard_map.64) | data formatting | bytes 1048576
